TPU v7x, 32 devices: a whole 2x2x4 slice. The times are simulated.
32 devices in a mesh: path: 8 (over z, y), land: 4 (over x, core).
Axes of the slice: x: 2, y: 2, z: 4, core: 2. Of those that a mesh axis runs over, the one named last changes fastest.
Arguments:
- state: float32 [50, 32768], P(None, 'path'), may hold values from -6 to 6
- next_value: float32 [32768], P('path'), may hold values from -6 to 6
- brownian: float32 [15, 32768], P(None, 'path'), may hold values from -6 to 6
- land_index: int32 [8192], P('land'), may hold values from 0 to 32767
Outputs:
- estimates: float32 [16, 32768], P(None, 'path')
All inputs are finite; a program needn't handle non-finite values.
Results may differ from a plain program's by a relative error of at most 0.0002.
Values sent between devices are 32-bit elements; how exact they have to be, the bound alone decides.
No kernel may reach another device: no remote copies, remote signals or barrier semaphores. Data moves between devices by JAX's collectives and lax.ppermute only.
A program may use at most 64 MiB of HBM per device.

v0:
```python
import math

import jax
import jax.numpy as jnp
from jax import lax
from jax.sharding import PartitionSpec as P

D = 50
M = 8192
ITERS = 2


LAMBDA_REG = 0.01


def features(rows, marks):
    cross = lax.dot_general(rows, marks, (((0,), (0,)), ((), ())), precision=lax.Precision.HIGHEST)
    dist = jnp.sum(rows * rows, 0)[:, None] + jnp.sum(marks * marks, 0)[None, :] - 2.0 * cross
    return jnp.exp(4.0 * (2.0 * D - jnp.maximum(dist, 0.0)) / D) / math.sqrt(M)


def split_rows(array, width):
    count = array.shape[1] // width
    return jnp.moveaxis(array.reshape(array.shape[0], count, width), 1, 0)


def forward_part(state, marks, coef):
    rows = state.shape[1]
    width = min(512, rows)

    def one(block):
        feat = features(block, marks)
        return lax.dot_general(
            coef, feat, (((1,), (1,)), ((), ())), precision=lax.Precision.HIGHEST
        )

    out = lax.map(one, split_rows(state, width))
    return jnp.moveaxis(out, 0, 1).reshape(coef.shape[0], rows)


def backward_part(state, marks, values):
    rows = state.shape[1]
    width = min(512, rows)

    def step(total, pair):
        feat = features(pair[0], marks)
        return (total + jnp.dot(pair[1], feat, precision=lax.Precision.HIGHEST), None)

    start = jnp.zeros((values.shape[0], marks.shape[1]), jnp.float32)
    total, unused = lax.scan(step, start, (split_rows(state, width), split_rows(values, width)))
    return total


def per_device(state, next_value, brownian, land_index):
    rows = state.shape[1]
    here = lax.axis_index("path")
    owner = land_index // rows
    column = land_index % rows
    picked = jnp.take(state, column, axis=1) * (owner == here).astype(jnp.float32)[None, :]
    marks = lax.psum(picked, "path")
    targets = jnp.concatenate([next_value[None, :], next_value[None, :] * brownian], 0)
    total_paths = rows * lax.axis_size("path")

    def spread(coef):
        return lax.psum(forward_part(state, marks, coef), "land")

    def pull_back(values):
        return lax.psum(backward_part(state, marks, values), "path") / total_paths

    def inner(values):
        return lax.psum(values, "land")

    rhs = pull_back(targets)
    coef = jnp.zeros_like(rhs)
    resid = rhs
    direction = rhs
    norm_now = inner(jnp.sum(resid * resid, 1))
    for step in range(ITERS):
        image = pull_back(spread(direction)) + LAMBDA_REG * direction
        alpha = norm_now / inner(jnp.sum(direction * image, 1))
        coef = coef + alpha[:, None] * direction
        resid = resid - alpha[:, None] * image
        norm_next = inner(jnp.sum(resid * resid, 1))
        direction = resid + (norm_next / norm_now)[:, None] * direction
        norm_now = norm_next
    return spread(coef)


def solution(mesh):
    in_specs = (P(None, "path"), P("path"), P(None, "path"), P("land"))
    out_specs = P(None, "path")
    return jax.shard_map(
        per_device, mesh=mesh, in_specs=in_specs, out_specs=out_specs, check_vma=False
    )
```

profile of v0, /device:TPU:0, one launch (start us, length us, event | category | flops | bytes accessed | tf_op | source)
XLA Modules:
  0.0 901.6 jit_solution(16363485892420364017)
XLA Ops:
  9.8 7.6 gather_fusion
  22.3 78.5 %all-reduce.9.cloned.1.call-done = f32[50,2048]{0,1:T(8,128)} async-done(((f32[50,2048]{0,1:T(8,128)}), f32[50,2048]{0,1:T(8,128)}) %all-reduce.9.cloned.1.call-update) | async-done | bytes 409616 | tf_op jit(solution)/shard_map/psum | solution.py:60
  104.0 85.0 %while.78 = (s32[]{:T(128)}, f32[16,2048]{1,0:T(8,128)S(1)}, f32[8,16,512]{2,0,1:T(8,128)S(1)}, f32[8,50,512]{2,1,0:T(8,128)S(1)}, f32[2048]{0:T(1024)S(1)}, /*index=5*/f32[50,2048]{1,0:T(8,128)S(1)}, s32[]{:T(128)}, s32[]{:T(128)}) while((s32[]{:T(128)}, f32[16,2048]{1,0:T(8,128)S(1)}, f32[8,16,512]{2,0,1:T(8,128)S(1)}, ...), condition=%wide.region_4.5_spmd.clone, body=%wide.region_2.4_spmd.clone.sunk | while | flops 837928448 | bytes 9437291 | solution.py:50
  189.9 69.1 %all-reduce.11.cloned.1.call-done = f32[16,2048]{1,0:T(8,128)} async-done(((f32[16,2048]{1,0:T(8,128)}), f32[16,2048]{1,0:T(8,128)}) %all-reduce.11.cloned.1.call-update) | async-done | bytes 131088 | tf_op jit(solution)/shard_map/psum | solution.py:68
  260.0 67.7 %while.75 = (s32[]{:T(128)}, f32[8,16,512]{2,1,0:T(8,128)S(1)}, f32[8,50,512]{2,1,0:T(8,128)S(1)}, f32[2048]{0:T(1024)S(1)}, f32[50,2048]{1,0:T(8,128)S(1)}, /*index=5*/f32[16,2048]{1,0:T(8,128)S(1)}, s32[]{:T(128)}) while((s32[]{:T(128)}, f32[8,16,512]{2,1,0:T(8,128)S(1)}, f32[8,50,512]{2,1,0:T(8,128)S(1)}, f32[2048]{0:T(1024)S(1)}, ...), condition=%wide.region_10.11_spmd, body=%wide.region_8.10_spmd.sunk | while | flops 837862912 | bytes 9240665 | solution.py:37
  328.7 31.1 %all-reduce.13.cloned.1.call-done = f32[8,16,512]{2,1,0:T(8,128)} async-done(((f32[8,16,512]{2,1,0:T(8,128)}), f32[8,16,512]{2,1,0:T(8,128)}) %all-reduce.13.cloned.1.call-update) | async-done | bytes 262160 | tf_op jit(solution)/shard_map/psum | solution.py:65
  359.8 84.9 %while.79 = (s32[]{:T(128)}, f32[16,2048]{1,0:T(8,128)S(1)}, f32[8,16,512]{2,1,0:T(8,128)}, f32[8,50,512]{2,1,0:T(8,128)S(1)}, f32[2048]{0:T(1024)S(1)}, /*index=5*/f32[50,2048]{1,0:T(8,128)S(1)}, s32[]{:T(128)}, s32[]{:T(128)}) while((s32[]{:T(128)}, f32[16,2048]{1,0:T(8,128)S(1)}, f32[8,16,512]{2,1,0:T(8,128)}, ...), condition=%wide.region_14.15_spmd.clone, body=%wide.region_12.14_spmd.clone.sunk | while | flops 837928448 | bytes 9372263 | solution.py:50
  364.8 5.5 fusion.276
  375.5 5.5 fusion.276
  386.1 5.5 fusion.276
  396.7 5.5 fusion.276
  407.3 5.5 fusion.276
  417.9 5.5 fusion.276
  428.5 5.5 fusion.276
  439.1 5.5 fusion.276
  445.4 69.7 %all-reduce.15.cloned.1.call-done = f32[16,2048]{1,0:T(8,128)} async-done(((f32[16,2048]{1,0:T(8,128)}), f32[16,2048]{1,0:T(8,128)}) %all-reduce.15.cloned.1.call-update) | async-done | bytes 131088 | tf_op jit(solution)/shard_map/psum | solution.py:68
  516.1 5.7 all-reduce
  522.9 6.8 psum.83
  530.8 67.7 %while.76 = (s32[]{:T(128)}, f32[8,16,512]{2,1,0:T(8,128)S(1)}, f32[8,50,512]{2,1,0:T(8,128)S(1)}, f32[2048]{0:T(1024)S(1)}, f32[50,2048]{1,0:T(8,128)S(1)}, /*index=5*/f32[16,2048]{1,0:T(8,128)S(1)}, s32[]{:T(128)}) while((s32[]{:T(128)}, f32[8,16,512]{2,1,0:T(8,128)S(1)}, f32[8,50,512]{2,1,0:T(8,128)S(1)}, f32[2048]{0:T(1024)S(1)}, ...), condition=%wide.region_22.23_spmd, body=%wide.region_20.22_spmd.sunk | while | flops 837862912 | bytes 9240665 | solution.py:37
  599.5 30.5 %all-reduce.17.cloned.1.call-done = f32[8,16,512]{2,1,0:T(8,128)} async-done(((f32[8,16,512]{2,1,0:T(8,128)}), f32[8,16,512]{2,1,0:T(8,128)}) %all-reduce.17.cloned.1.call-update) | async-done | bytes 262160 | tf_op jit(solution)/shard_map/psum | solution.py:65
  630.0 84.8 %while.80 = (s32[]{:T(128)}, f32[16,2048]{1,0:T(8,128)S(1)}, f32[8,16,512]{2,1,0:T(8,128)}, f32[8,50,512]{2,1,0:T(8,128)S(1)}, f32[2048]{0:T(1024)S(1)}, /*index=5*/f32[50,2048]{1,0:T(8,128)S(1)}, s32[]{:T(128)}, s32[]{:T(128)}) while((s32[]{:T(128)}, f32[16,2048]{1,0:T(8,128)S(1)}, f32[8,16,512]{2,1,0:T(8,128)}, ...), condition=%wide.region_26.27_spmd.clone, body=%wide.region_24.26_spmd.clone.sunk | while | flops 837928448 | bytes 9372263 | solution.py:50
  635.1 5.5 fusion.283
  645.7 5.5 fusion.283
  666.9 5.5 fusion.283
  677.5 5.5 fusion.283
  688.1 5.5 fusion.283
  698.7 5.5 fusion.283
  709.3 5.5 fusion.283
  715.6 69.7 %all-reduce.19.cloned.1.call-done = f32[16,2048]{1,0:T(8,128)} async-done(((f32[16,2048]{1,0:T(8,128)}), f32[16,2048]{1,0:T(8,128)}) %all-reduce.19.cloned.1.call-update) | async-done | bytes 131088 | tf_op jit(solution)/shard_map/psum | solution.py:68
  786.3 6.0 psum.86
  792.4 67.6 %while.77 = (s32[]{:T(128)}, f32[8,16,512]{2,1,0:T(8,128)S(1)}, f32[8,50,512]{2,1,0:T(8,128)S(1)}, f32[2048]{0:T(1024)S(1)}, f32[50,2048]{1,0:T(8,128)S(1)}, /*index=5*/f32[16,2048]{1,0:T(8,128)S(1)}, s32[]{:T(128)}) while((s32[]{:T(128)}, f32[8,16,512]{2,1,0:T(8,128)S(1)}, f32[8,50,512]{2,1,0:T(8,128)S(1)}, f32[2048]{0:T(1024)S(1)}, ...), condition=%wide.region_32.33_spmd, body=%wide.region_30.32_spmd.sunk | while | flops 837862912 | bytes 9240665 | solution.py:37
  860.8 31.6 %all-reduce.21.cloned.1.call-done = f32[16,4096]{1,0:T(8,128)} async-done(((f32[16,4096]{1,0:T(8,128)}), f32[16,4096]{1,0:T(8,128)}) %all-reduce.21.cloned.1.call-update) | async-done | bytes 262160 | tf_op jit(solution)/shard_map/psum | solution.py:65
  (198 shorter events, 397.6 us)
Async XLA Ops:
  6.5 94.3 %all-reduce.9.cloned.1.call-start = ((), (), s32[]{:S(2)}) async-start(), calls=%async_computation | async-start | bytes 2097152 | tf_op jit(solution)/shard_map/psum | solution.py:60
  9.8 10.2 %copy-start.7 = (f32[4096]{0:T(1024)S(1)}, f32[4096]{0:T(1024)}, u32[]{:S(2)}) copy-start(f32[4096]{0:T(1024)} %param.17) | copy-start | bytes 49156
  9.8 11.2 %copy-start = (f32[50,4096]{1,0:T(8,128)S(1)}, f32[50,4096]{1,0:T(8,128)}, u32[]{:S(2)}) copy-start(f32[50,4096]{1,0:T(8,128)} %param.16) | copy-start | bytes 2457604
  20.0 239.1 %all-reduce.11.cloned.1.call-start = ((), (), s32[]{:S(2)}) async-start(), calls=%async_computation.1 | async-start | bytes 262144 | tf_op jit(solution)/shard_map/psum | solution.py:68
  189.0 0.7 copy-start.4
  189.7 170.1 %all-reduce.13.cloned.1.call-start = ((), (), s32[]{:S(2)}) async-start(), calls=%async_computation.2 | async-start | bytes 524288 | tf_op jit(solution)/shard_map/psum | solution.py:65
  327.7 0.7 copy-start.2
  328.4 186.7 %all-reduce.15.cloned.1.call-start = ((), (), s32[]{:S(2)}) async-start(), calls=%async_computation.3 | async-start | bytes 262144 | tf_op jit(solution)/shard_map/psum | solution.py:68
  359.8 155.3 %copy-start.1 = (f32[16,2048]{1,0:T(8,128)S(1)}, f32[16,2048]{1,0:T(8,128)}, u32[]{:S(2)}) copy-start(f32[16,2048]{1,0:T(8,128)} %all-reduce.11.cloned.1.call-done) | copy-start | bytes 393220
  444.6 0.7 copy-start.5
  445.3 184.7 %all-reduce.17.cloned.1.call-start = ((), (), s32[]{:S(2)}) async-start(), calls=%async_computation.4 | async-start | bytes 524288 | tf_op jit(solution)/shard_map/psum | solution.py:65
  598.4 0.7 copy-start.3
  599.2 186.1 %all-reduce.19.cloned.1.call-start = ((), (), s32[]{:S(2)}) async-start(), calls=%async_computation.5 | async-start | bytes 262144 | tf_op jit(solution)/shard_map/psum | solution.py:68
  714.8 0.7 copy-start.6
  715.5 177.0 %all-reduce.21.cloned.1.call-start = ((), (), s32[]{:S(2)}) async-start(), calls=%async_computation.6 | async-start | bytes 524288 | tf_op jit(solution)/shard_map/psum | solution.py:65
Sparse Core Ops, SparseCore 0:
  20.1 80.7 all-reduce.8
  189.8 69.1 all-reduce.10
  328.5 31.2 all-reduce.12
  445.5 69.5 all-reduce.14
  599.3 30.6 all-reduce.16
  715.6 69.5 all-reduce.18
  861.0 31.4 all-reduce.20
where the time goes:
time: 908 us; the launch traced here: 902 us
  matrix products  455 us (50%)
  waiting for transfers between devices  380 us (42%)
  blocking collectives  18.5 us (2%)
  local copies, waits for them, and re-layouts  18.3 us (2%)
  between operations  14.2 us (2%)
  other arithmetic  13.3 us (1%)
    psum x3, waiting for transfers between devices, pull_back(): return lax.psum(backward_part(state, marks, values), 'path') / total_paths  209 us
    dot_general x48, matrix products, features(): lax.dot_general(rows, marks, (((0,), (0,)), ((), ())), precision=lax.Prec...  206 us
    dot_general x24, matrix products, step(): jnp.dot(pair[1], feat, precision=lax.Precision.HIGHEST)  132 us
    dot_general x24, matrix products, one(): lax.dot_general(coef, feat, (((1,), (1,)), ((), ())), precision=lax.Preci...  117 us
    psum x3, waiting for transfers between devices, spread(): return lax.psum(forward_part(state, marks, coef), 'land')  93.2 us
    psum x1, waiting for transfers between devices, per_device(): marks = lax.psum(picked, 'path')  78.5 us
    psum x3, blocking collectives, inner(): return lax.psum(values, 'land')  18.5 us
  transfers between devices with their start and end apart: 7, of which 7 were waited for; matrix products, arithmetic and copies ran while one was open for 0% of the time, Pallas kernels for 0%

commit v1 on v0

v1 whole, which is shorter than its diff:
```python
import math

import jax
import jax.numpy as jnp
from jax import lax
from jax.experimental import pallas as pl
from jax.experimental.pallas import tpu as pltpu
from jax.sharding import PartitionSpec as P

LAMBDA_REG = 0.01
LOG2E = 1.4426950408889634
DEPTH = 256
BAND = DEPTH // 4
WHOLE = pl.BlockSpec(memory_space=pltpu.VMEM)
BF16, F32 = jnp.bfloat16, jnp.float32


def pieces(x, count):
    out = []
    for unused in range(count):
        part = x.astype(BF16).astype(F32)
        out.append(part)
        x = x - part
    return out


def augment(ref, x, top, of_path):
    dims, count = x.shape
    rate = 4.0 * LOG2E / dims
    norm = -rate * jnp.sum(x * x, 0, keepdims=True)
    ones = jnp.ones((1, count), F32)
    if of_path:
        high, low = pieces(x * (2.0 * rate), 2)
        bands = (high, high, low, low)
        extra = pieces(norm + top, 3) + [ones] * 3
    else:
        high, low = pieces(x, 2)
        bands = (high, low, high, low)
        extra = [ones] * 3 + pieces(norm, 3)
    ref[...] = jnp.zeros_like(ref)
    for place, band in enumerate(bands):
        ref[place * BAND : place * BAND + dims, :] = band
    for place, row in enumerate(extra):
        ref[dims + place : dims + place + 1, :] = row


def prepare(x, top, of_path):
    count = x.shape[1]

    def kernel(x_ref, out_ref, turned_ref, full):
        augment(full, x_ref[...], top, of_path)
        step = min(512, count)
        for start in range(0, count, step):
            block = full[:, start : start + step]
            out_ref[:, start : start + step] = block.astype(BF16)
            turned_ref[start : start + step, :] = block.T.astype(BF16)

    return pl.pallas_call(
        kernel,
        in_specs=[WHOLE],
        out_specs=[WHOLE, WHOLE],
        out_shape=[
            jax.ShapeDtypeStruct((DEPTH, count), BF16),
            jax.ShapeDtypeStruct((count, DEPTH), BF16),
        ],
        scratch_shapes=[pltpu.VMEM((DEPTH, count), F32)],
        compiler_params=pltpu.CompilerParams(vmem_limit_bytes=40 * 2**20),
        name="prepare",
    )(x)


def apply_features(left, right, values, other, top):
    depth, width = left.shape[0], right.shape[1]
    rows = values.shape[0]
    tile = min(512, depth)
    span = min(1024, width)

    def kernel(left_ref, right_ref, values_ref, other_ref, out_ref):
        v = values_ref[...]
        square = jnp.sum(v * v, 1, keepdims=True)
        mixed = jnp.sum(v * other_ref[...], 1, keepdims=True)
        lane = lax.broadcasted_iota(jnp.int32, (rows, 128), 1)
        out_ref[:, width:] = jnp.where(lane < 64, square, mixed)
        out_ref[:, :width] = jnp.zeros((rows, width), F32)

        @pl.loop(0, depth // tile)
        def _(i):
            at = pl.ds(pl.multiple_of(i * tile, tile), tile)
            part = values_ref[:, at]
            part_high = part.astype(BF16)
            part_low = (part - part_high.astype(F32)).astype(BF16)
            both = jnp.concatenate([part_high, part_low], 0)
            for start in range(0, width, span):
                exponent = jnp.dot(
                    left_ref[at, :], right_ref[:, start : start + span], preferred_element_type=F32
                )
                feat = jnp.exp2(jnp.minimum(exponent, top))
                high = feat.astype(BF16)
                low = (feat - high.astype(F32)).astype(BF16)
                first = jnp.dot(both, high, preferred_element_type=F32)
                second = jnp.dot(part_high, low, preferred_element_type=F32)
                out_ref[:, start : start + span] += first[:rows] + first[rows:] + second

    return pl.pallas_call(
        kernel,
        in_specs=[WHOLE] * 4,
        out_specs=WHOLE,
        out_shape=jax.ShapeDtypeStruct((rows, width + 128), F32),
        compiler_params=pltpu.CompilerParams(vmem_limit_bytes=40 * 2**20),
        name="apply_features",
    )(left, right, values, other)


def swap(x, axis, bit):
    count = lax.axis_size(axis)
    return lax.ppermute(x, axis, [(i, i ^ bit) for i in range(count)])


def bits(axis):
    out, bit = [], 1
    while bit < lax.axis_size(axis):
        out.append(bit)
        bit *= 2
    return out


def total(x, axis):
    for bit in bits(axis):
        x = x + swap(x, axis, bit)
    return x


def total_by_halves(x, axis):
    here = lax.axis_index(axis)
    for bit in bits(axis):
        half = x.shape[1] // 2
        upper = (here & bit) != 0
        keep = jnp.where(upper, x[:, half:], x[:, :half])
        send = jnp.where(upper, x[:, :half], x[:, half:])
        x = keep + swap(send, axis, bit)
    for bit in reversed(bits(axis)):
        upper = (here & bit) != 0
        other = swap(x, axis, bit)
        x = jnp.where(
            upper, jnp.concatenate([other, x], 1), jnp.concatenate([x, other], 1)
        )
    return x


def per_device(state, next_value, brownian, land_index):
    rows = state.shape[1]
    lands = land_index.shape[0]
    paths = rows * lax.axis_size("path")
    landmarks = lands * lax.axis_size("land")
    top = 8.0 * LOG2E - 0.5 * math.log2(landmarks)

    here = lax.axis_index("path")
    owner = land_index // rows
    picked = jnp.take(state, land_index % rows, axis=1)
    picked = jnp.where((owner == here)[None, :], picked, 0.0)
    marks = total_by_halves(picked, "path")

    path_right, path_left = prepare(state, top, True)
    mark_right, mark_left = prepare(marks, top, False)
    targets = jnp.concatenate([next_value[None, :], next_value[None, :] * brownian], 0)

    def pull_back(values):
        return total(apply_features(path_left, mark_right, values, values, top), "path")

    def spread(values, other):
        return total(apply_features(mark_left, path_right, values, other, top), "land")

    rhs = pull_back(targets)[:, :lands] / paths
    spread_rhs = spread(rhs, rhs)
    first = spread_rhs[:, :rows]
    norm = spread_rhs[:, rows : rows + 1]
    back = pull_back(first)
    image = back[:, :lands] / paths + LAMBDA_REG * rhs
    alpha = norm / (back[:, lands : lands + 1] / paths + LAMBDA_REG * norm)
    resid = rhs - alpha * image
    spread_resid = spread(resid, rhs)
    norm_next = spread_resid[:, rows : rows + 1]
    mixed = spread_resid[:, rows + 64 : rows + 65]
    beta = norm_next / norm
    second = spread_resid[:, :rows] + beta * first
    squares = total(
        jnp.broadcast_to(jnp.sum(second * second, 1, keepdims=True), (second.shape[0], 128)), "path"
    )[:, :1]
    length = norm_next + 2.0 * beta * mixed + beta * beta * norm
    alpha_next = norm_next / (squares / paths + LAMBDA_REG * length)
    return alpha * first + alpha_next * second


def solution(mesh):
    in_specs = (P(None, "path"), P("path"), P(None, "path"), P("land"))
    out_specs = P(None, "path")
    return jax.shard_map(
        per_device, mesh=mesh, in_specs=in_specs, out_specs=out_specs, check_vma=False
    )
```

time: 908 us -> 160 us (0.18)
  matrix products: 455 us -> 0 us
  waiting for transfers between devices: 380 us -> 61.9 us
  Pallas kernels: 0 us -> 46.7 us
  starting transfers between devices: 0.93 us -> 39.2 us
  blocking collectives: 18.5 us -> 0 us
  between operations: 14.2 us -> 0.2 us
  local copies, waits for them, and re-layouts: 18.3 us -> 7.75 us
  other arithmetic: 13.3 us -> 3.68 us
    dot_general x96 -> x0, matrix products: 455 us -> none  [the longest x48 206 us: features(): lax.dot_general(rows, marks, (((0,), (0,)), ((), ())), precision=lax.Prec...]
    psum x7 -> x0, waiting for transfers between devices: 380 us -> none  [the longest x3 209 us: pull_back(): return lax.psum(backward_part(state, marks, values), 'path') / total_paths]
    ppermute x0 -> x19, waiting for transfers between devices: none -> 61.9 us  [swap(): return lax.ppermute(x, axis, [(i, i ^ bit) for i in range(count)])]
    pallas_call x0 -> x6, Pallas kernels: none -> 46.7 us  [the longest x4 45.3 us: apply_features(): pl.pallas_call(kernel, in_specs=[WHOLE] * 4, out_specs=WHOLE, out_shape=j...]
    ppermute x0 -> x19, starting transfers between devices: none -> 39.2 us  [swap(): return lax.ppermute(x, axis, [(i, i ^ bit) for i in range(count)])]
    psum x3 -> x0, blocking collectives: 18.5 us -> none  [inner(): return lax.psum(values, 'land')]
  transfers between devices with their start and end apart: 7 -> 19, of which waited for: 7 -> 19; matrix products, arithmetic and copies ran while one was open for 0% -> 0% of each run, Pallas kernels for 0% -> 1%
where the time goes in v1:
time: 160 us; the launch traced here: 159 us
  waiting for transfers between devices  61.9 us (39%)
  Pallas kernels  46.7 us (29%)
  starting transfers between devices  39.2 us (25%)
  local copies, waits for them, and re-layouts  7.75 us (5%)
  other arithmetic  3.68 us (2%)
    ppermute x19, waiting for transfers between devices, swap(): return lax.ppermute(x, axis, [(i, i ^ bit) for i in range(count)])  61.9 us
    pallas_call x4, Pallas kernels, apply_features(): pl.pallas_call(kernel, in_specs=[WHOLE] * 4, out_specs=WHOLE, out_shape=j...  45.3 us
    ppermute x19, starting transfers between devices, swap(): return lax.ppermute(x, axis, [(i, i ^ bit) for i in range(count)])  39.2 us
    gather x2, local copies, waits for them, and re-layouts, per_device(): picked = jnp.take(state, land_index % rows, axis=1)  5.82 us
  transfers between devices with their start and end apart: 19, of which 19 were waited for; matrix products, arithmetic and copies ran while one was open for 0% of the time, Pallas kernels for 1%

profile of v1, /device:TPU:0, one launch (start us, length us, event | category | flops | bytes accessed | tf_op | source)
XLA Modules:
  0.0 159.4 jit_solution(8393152666332012765)
XLA Ops:
  1.4 1.8 %copy.7 = f32[50,4096]{0,1:T(8,128)S(1)} copy(f32[50,4096]{1,0:T(8,128)} %x_ref.1) | data formatting | bytes 1638400 | tf_op args[0]
  3.3 5.5 %gather_fusion = f32[2048,50]{1,0:T(8,128)S(1)} fusion(f32[50,4096]{0,1:T(8,128)S(1)} %copy.7, s32[2048]{0:T(1024)S(1)} %broadcast_clamp_fusion), kind=kCustom, calls=%fused_computation | custom fusion | bytes 827392 | tf_op jit(solution)/shard_map/jit(_take)/gather | solution.py:159
  9.2 3.0 %collective-permute-start = (f32[50,1024]{1,0:T(8,128)S(1)}, f32[50,1024]{1,0:T(8,128)S(1)}, u32[]{:S(2)}, u32[]{:S(2)}) collective-permute-start(f32[50,1024]{1,0:T(8,128)S(1)} %slice_select_fusion), channel_id=1, source_target_pairs={{0,4},{4,0},{8,12},{12,8},{16,20},{20,16},{24,28},{28,24},{1,5},{5... | collective-permute-start | bytes 614408 | tf_op jit(solution)/shard_map/ppermute | solution.py:116
  12.2 5.6 %collective-permute-done = f32[50,1024]{1,0:T(8,128)S(1)} collective-permute-done((f32[50,1024]{1,0:T(8,128)S(1)}, f32[50,1024]{1,0:T(8,128)S(1)}, u32[]{:S(2)}, u32[]{:S(2)}) %collective-permute-start) | collective-permute-done | bytes 204832 | tf_op jit(solution)/shard_map/ppermute | solution.py:116
  17.9 1.9 %collective-permute-start.1 = (f32[50,512]{1,0:T(8,128)S(1)}, f32[50,512]{1,0:T(8,128)S(1)}, u32[]{:S(2)}, u32[]{:S(2)}) collective-permute-start(f32[50,512]{1,0:T(8,128)S(1)} %slice_select_fusion.1), channel_id=1, source_target_pairs={{0,8},{4,12},{8,0},{12,4},{16,24},{20,28},{24,16},{28,20},{1,9},{5... | collective-permute-start | bytes 307208 | tf_op jit(solution)/shard_map/ppermute | solution.py:116
  19.8 3.0 %collective-permute-done.1 = f32[50,512]{1,0:T(8,128)S(1)} collective-permute-done((f32[50,512]{1,0:T(8,128)S(1)}, f32[50,512]{1,0:T(8,128)S(1)}, u32[]{:S(2)}, u32[]{:S(2)}) %collective-permute-start.1) | collective-permute-done | bytes 102432 | tf_op jit(solution)/shard_map/ppermute | solution.py:116
  22.8 2.9 %collective-permute-start.2 = (f32[50,256]{1,0:T(8,128)S(1)}, f32[50,256]{1,0:T(8,128)S(1)}, u32[]{:S(2)}, u32[]{:S(2)}) collective-permute-start(f32[50,256]{1,0:T(8,128)S(1)} %slice_select_fusion.2), channel_id=1, source_target_pairs={{0,16},{4,20},{8,24},{12,28},{16,0},{20,4},{24,8},{28,12},{1,17},{... | collective-permute-start | bytes 153608 | tf_op jit(solution)/shard_map/ppermute | solution.py:116
  25.7 2.3 %collective-permute-done.2 = f32[50,256]{1,0:T(8,128)S(1)} collective-permute-done((f32[50,256]{1,0:T(8,128)S(1)}, f32[50,256]{1,0:T(8,128)S(1)}, u32[]{:S(2)}, u32[]{:S(2)}) %collective-permute-start.2) | collective-permute-done | bytes 51232 | tf_op jit(solution)/shard_map/ppermute | solution.py:116
  28.0 2.9 %collective-permute-start.3 = (f32[50,256]{1,0:T(8,128)S(1)}, f32[50,256]{1,0:T(8,128)S(1)}, u32[]{:S(2)}, u32[]{:S(2)}) collective-permute-start(f32[50,256]{1,0:T(8,128)S(1)} %select_add_fusion.2), channel_id=1, source_target_pairs={{0,16},{4,20},{8,24},{12,28},{16,0},{20,4},{24,8},{28,12},{1,17},{... | collective-permute-start | bytes 153608 | tf_op jit(solution)/shard_map/ppermute | solution.py:116
  30.9 2.3 %collective-permute-done.3 = f32[50,256]{1,0:T(8,128)S(1)} collective-permute-done((f32[50,256]{1,0:T(8,128)S(1)}, f32[50,256]{1,0:T(8,128)S(1)}, u32[]{:S(2)}, u32[]{:S(2)}) %collective-permute-start.3) | collective-permute-done | bytes 51232 | tf_op jit(solution)/shard_map/ppermute | solution.py:116
  33.2 3.4 %collective-permute-start.4 = (f32[50,512]{1,0:T(8,128)S(1)}, f32[50,512]{1,0:T(8,128)S(1)}, u32[]{:S(2)}, u32[]{:S(2)}) collective-permute-start(f32[50,512]{1,0:T(8,128)S(1)} %maximum_select_fusion.2), channel_id=1, source_target_pairs={{0,8},{4,12},{8,0},{12,4},{16,24},{20,28},{24,16},{28,20},{1,9},{5... | collective-permute-start | bytes 307208 | tf_op jit(solution)/shard_map/ppermute | solution.py:116
  36.7 2.7 %collective-permute-done.4 = f32[50,512]{1,0:T(8,128)S(1)} collective-permute-done((f32[50,512]{1,0:T(8,128)S(1)}, f32[50,512]{1,0:T(8,128)S(1)}, u32[]{:S(2)}, u32[]{:S(2)}) %collective-permute-start.4) | collective-permute-done | bytes 102432 | tf_op jit(solution)/shard_map/ppermute | solution.py:116
  42.0 3.6 %collective-permute-done.5 = f32[50,1024]{1,0:T(8,128)S(1)} collective-permute-done((f32[50,1024]{1,0:T(8,128)S(1)}, f32[50,1024]{1,0:T(8,128)S(1)}, u32[]{:S(2)}, u32[]{:S(2)}) %collective-permute-start.5) | collective-permute-done | bytes 204832 | tf_op jit(solution)/shard_map/ppermute | solution.py:116
  46.1 11.5 %apply_features.4 = f32[16,2176]{1,0:T(8,128)S(1)} custom-call(bf16[4096,256]{1,0:T(8,128)(2,1)S(1)} %get-tuple-element.11.left_ref, bf16[256,2048]{1,0:T(8,128)(2,1)S(1)} %get-tuple-element.12.right_ref, f32[16,4096]{1,0:T(8,128)S(1)} %pad_maximum_fusion.values_ref.other_ref, f32[16,4096]{1,0:T(8,128)S(1)} %pad_maximum_fusion.values_ref.other_ref), custom_call_target="tpu_custom_call" | custom-call | tf_op jit(solution)/shard_map/apply_features/pallas_call | solution.py:104
  59.1 3.5 %collective-permute-done.6 = f32[16,2176]{1,0:T(8,128)S(1)} collective-permute-done((f32[16,2176]{1,0:T(8,128)S(1)}, f32[16,2176]{1,0:T(8,128)S(1)}, u32[]{:S(2)}, u32[]{:S(2)}) %collective-permute-start.6) | collective-permute-done | bytes 139296 | tf_op jit(solution)/shard_map/ppermute | solution.py:116
  62.6 2.1 %collective-permute-start.7 = (f32[16,2176]{1,0:T(8,128)S(1)}, f32[16,2176]{1,0:T(8,128)S(1)}, u32[]{:S(2)}, u32[]{:S(2)}) collective-permute-start(f32[16,2176]{1,0:T(8,128)S(1)} %add.87), channel_id=1, source_target_pairs={{0,8},{4,12},{8,0},{12,4},{16,24},{20,28},{24,16},{28,20},{1,9},{5... | collective-permute-start | bytes 417800 | tf_op jit(solution)/shard_map/ppermute | solution.py:116
  64.7 3.0 %collective-permute-done.7 = f32[16,2176]{1,0:T(8,128)S(1)} collective-permute-done((f32[16,2176]{1,0:T(8,128)S(1)}, f32[16,2176]{1,0:T(8,128)S(1)}, u32[]{:S(2)}, u32[]{:S(2)}) %collective-permute-start.7) | collective-permute-done | bytes 139296 | tf_op jit(solution)/shard_map/ppermute | solution.py:116
  67.8 2.4 %collective-permute-start.8 = (f32[16,2176]{1,0:T(8,128)S(1)}, f32[16,2176]{1,0:T(8,128)S(1)}, u32[]{:S(2)}, u32[]{:S(2)}) collective-permute-start(f32[16,2176]{1,0:T(8,128)S(1)} %add.88), channel_id=1, source_target_pairs={{0,16},{4,20},{8,24},{12,28},{16,0},{20,4},{24,8},{28,12},{1,17},{... | collective-permute-start | bytes 417800 | tf_op jit(solution)/shard_map/ppermute | solution.py:116
  70.2 3.6 %collective-permute-done.8 = f32[16,2176]{1,0:T(8,128)S(1)} collective-permute-done((f32[16,2176]{1,0:T(8,128)S(1)}, f32[16,2176]{1,0:T(8,128)S(1)}, u32[]{:S(2)}, u32[]{:S(2)}) %collective-permute-start.8) | collective-permute-done | bytes 139296 | tf_op jit(solution)/shard_map/ppermute | solution.py:116
  73.8 11.2 %apply_features.5 = f32[16,4224]{1,0:T(8,128)S(1)} custom-call(bf16[2048,256]{1,0:T(8,128)(2,1)S(1)} %get-tuple-element.9.left_ref, bf16[256,4096]{1,0:T(8,128)(2,1)S(1)} %get-tuple-element.10.right_ref, f32[16,2048]{1,0:T(8,128)S(1)} %broadcast_multiply_fusion.1.values_ref.other_ref, f32[16,2048]{1,0:T(8,128)S(1)} %broadcast_multiply_fusion.1.values_ref.other_ref), custom_call_target="tpu_custom_call" | custom-call | tf_op jit(solution)/shard_map/apply_features/pallas_call | solution.py:104
  88.1 7.0 %collective-permute-done.10 = f32[16,4224]{1,0:T(8,128)S(1)} collective-permute-done((f32[16,4224]{1,0:T(8,128)S(1)}, f32[16,4224]{1,0:T(8,128)S(1)}, u32[]{:S(2)}, u32[]{:S(2)}) %collective-permute-start.10) | collective-permute-done | bytes 270368 | tf_op jit(solution)/shard_map/ppermute | solution.py:116
  95.2 11.5 %apply_features.6 = f32[16,2176]{1,0:T(8,128)S(1)} custom-call(bf16[4096,256]{1,0:T(8,128)(2,1)S(1)} %get-tuple-element.11.left_ref, bf16[256,2048]{1,0:T(8,128)(2,1)S(1)} %get-tuple-element.12.right_ref, f32[16,4096]{1,0:T(8,128)S(1)} %slice.77.values_ref.other_ref, f32[16,4096]{1,0:T(8,128)S(1)} %slice.77.values_ref.other_ref), custom_call_target="tpu_custom_call" | custom-call | tf_op jit(solution)/shard_map/apply_features/pallas_call | solution.py:104
  108.3 3.5 %collective-permute-done.11 = f32[16,2176]{1,0:T(8,128)S(1)} collective-permute-done((f32[16,2176]{1,0:T(8,128)S(1)}, f32[16,2176]{1,0:T(8,128)S(1)}, u32[]{:S(2)}, u32[]{:S(2)}) %collective-permute-start.11) | collective-permute-done | bytes 139296 | tf_op jit(solution)/shard_map/ppermute | solution.py:116
  111.8 2.1 %collective-permute-start.12 = (f32[16,2176]{1,0:T(8,128)S(1)}, f32[16,2176]{1,0:T(8,128)S(1)}, u32[]{:S(2)}, u32[]{:S(2)}) collective-permute-start(f32[16,2176]{1,0:T(8,128)S(1)} %add.92), channel_id=1, source_target_pairs={{0,8},{4,12},{8,0},{12,4},{16,24},{20,28},{24,16},{28,20},{1,9},{5... | collective-permute-start | bytes 417800 | tf_op jit(solution)/shard_map/ppermute | solution.py:116
  113.9 3.0 %collective-permute-done.12 = f32[16,2176]{1,0:T(8,128)S(1)} collective-permute-done((f32[16,2176]{1,0:T(8,128)S(1)}, f32[16,2176]{1,0:T(8,128)S(1)}, u32[]{:S(2)}, u32[]{:S(2)}) %collective-permute-start.12) | collective-permute-done | bytes 139296 | tf_op jit(solution)/shard_map/ppermute | solution.py:116
  117.0 3.3 %collective-permute-start.13 = (f32[16,2176]{1,0:T(8,128)S(1)}, f32[16,2176]{1,0:T(8,128)S(1)}, u32[]{:S(2)}, u32[]{:S(2)}) collective-permute-start(f32[16,2176]{1,0:T(8,128)S(1)} %add.93), channel_id=1, source_target_pairs={{0,16},{4,20},{8,24},{12,28},{16,0},{20,4},{24,8},{28,12},{1,17},{... | collective-permute-start | bytes 417800 | tf_op jit(solution)/shard_map/ppermute | solution.py:116
  120.3 3.0 %collective-permute-done.13 = f32[16,2176]{1,0:T(8,128)S(1)} collective-permute-done((f32[16,2176]{1,0:T(8,128)S(1)}, f32[16,2176]{1,0:T(8,128)S(1)}, u32[]{:S(2)}, u32[]{:S(2)}) %collective-permute-start.13) | collective-permute-done | bytes 139296 | tf_op jit(solution)/shard_map/ppermute | solution.py:116
  123.6 11.2 %apply_features.7 = f32[16,4224]{1,0:T(8,128)S(1)} custom-call(bf16[2048,256]{1,0:T(8,128)(2,1)S(1)} %get-tuple-element.9.left_ref, bf16[256,4096]{1,0:T(8,128)(2,1)S(1)} %get-tuple-element.10.right_ref, f32[16,2048]{1,0:T(8,128)S(1)} %fusion.2.values_ref, f32[16,2048]{1,0:T(8,128)S(1)} %broadcast_multiply_fusion.1.values_ref.other_ref), custom_call_target="tpu_custom_call" | custom-call | tf_op jit(solution)/shard_map/apply_features/pallas_call | solution.py:104
  137.9 7.0 %collective-permute-done.15 = f32[16,4224]{1,0:T(8,128)S(1)} collective-permute-done((f32[16,4224]{1,0:T(8,128)S(1)}, f32[16,4224]{1,0:T(8,128)S(1)}, u32[]{:S(2)}, u32[]{:S(2)}) %collective-permute-start.15) | collective-permute-done | bytes 270368 | tf_op jit(solution)/shard_map/ppermute | solution.py:116
  146.9 2.1 %collective-permute-done.16 = f32[16,128]{1,0:T(8,128)S(1)} collective-permute-done((f32[16,128]{1,0:T(8,128)S(1)}, f32[16,128]{1,0:T(8,128)S(1)}, u32[]{:S(2)}, u32[]{:S(2)}) %collective-permute-start.16) | collective-permute-done | bytes 8224 | tf_op jit(solution)/shard_map/ppermute | solution.py:116
  149.1 2.5 %collective-permute-start.17 = (f32[16,128]{1,0:T(8,128)S(1)}, f32[16,128]{1,0:T(8,128)S(1)}, u32[]{:S(2)}, u32[]{:S(2)}) collective-permute-start(f32[16,128]{1,0:T(8,128)S(1)} %broadcast_add_fusion), channel_id=1, source_target_pairs={{0,8},{4,12},{8,0},{12,4},{16,24},{20,28},{24,16},{28,20},{1,9},{5... | collective-permute-start | bytes 24584 | tf_op jit(solution)/shard_map/ppermute | solution.py:116
  153.3 3.5 %collective-permute-start.18 = (f32[16,128]{1,0:T(8,128)S(1)}, f32[16,128]{1,0:T(8,128)S(1)}, u32[]{:S(2)}, u32[]{:S(2)}) collective-permute-start(f32[16,128]{1,0:T(8,128)S(1)} %fusion.17), channel_id=1, source_target_pairs={{0,16},{4,20},{8,24},{12,28},{16,0},{20,4},{24,8},{28,12},{1,17},{... | collective-permute-start | bytes 24584 | tf_op jit(solution)/shard_map/ppermute | solution.py:116
  (55 shorter events, 21.1 us)
Async XLA Ops:
  9.1 27.6 %copy-start.1 = (f32[15,4096]{1,0:T(8,128)S(1)}, f32[15,4096]{1,0:T(8,128)}, u32[]{:S(2)}) copy-start(f32[15,4096]{1,0:T(8,128)} %param.6) | copy-start | bytes 737284
  9.1 27.6 %copy-start.2 = (f32[4096]{0:T(1024)S(1)}, f32[4096]{0:T(1024)}, u32[]{:S(2)}) copy-start(f32[4096]{0:T(1024)} %param.5) | copy-start | bytes 49156
  9.2 31.9 %copy-start = (f32[50,4096]{1,0:T(8,128)S(1)}, f32[50,4096]{1,0:T(8,128)}, u32[]{:S(2)}) copy-start(f32[50,4096]{1,0:T(8,128)} %x_ref.1) | copy-start | bytes 2457604
  9.2 8.6 %collective-permute-start = (f32[50,1024]{1,0:T(8,128)S(1)}, f32[50,1024]{1,0:T(8,128)S(1)}, u32[]{:S(2)}, u32[]{:S(2)}) collective-permute-start(f32[50,1024]{1,0:T(8,128)S(1)} %slice_select_fusion), channel_id=1, source_target_pairs={{0,4},{4,0},{8,12},{12,8},{16,20},{20,16},{24,28},{28,24},{1,5},{5... | collective-permute-start | bytes 614408 | tf_op jit(solution)/shard_map/ppermute | solution.py:116
  17.9 4.9 %collective-permute-start.1 = (f32[50,512]{1,0:T(8,128)S(1)}, f32[50,512]{1,0:T(8,128)S(1)}, u32[]{:S(2)}, u32[]{:S(2)}) collective-permute-start(f32[50,512]{1,0:T(8,128)S(1)} %slice_select_fusion.1), channel_id=1, source_target_pairs={{0,8},{4,12},{8,0},{12,4},{16,24},{20,28},{24,16},{28,20},{1,9},{5... | collective-permute-start | bytes 307208 | tf_op jit(solution)/shard_map/ppermute | solution.py:116
  22.8 5.1 %collective-permute-start.2 = (f32[50,256]{1,0:T(8,128)S(1)}, f32[50,256]{1,0:T(8,128)S(1)}, u32[]{:S(2)}, u32[]{:S(2)}) collective-permute-start(f32[50,256]{1,0:T(8,128)S(1)} %slice_select_fusion.2), channel_id=1, source_target_pairs={{0,16},{4,20},{8,24},{12,28},{16,0},{20,4},{24,8},{28,12},{1,17},{... | collective-permute-start | bytes 153608 | tf_op jit(solution)/shard_map/ppermute | solution.py:116
  28.0 5.2 %collective-permute-start.3 = (f32[50,256]{1,0:T(8,128)S(1)}, f32[50,256]{1,0:T(8,128)S(1)}, u32[]{:S(2)}, u32[]{:S(2)}) collective-permute-start(f32[50,256]{1,0:T(8,128)S(1)} %select_add_fusion.2), channel_id=1, source_target_pairs={{0,16},{4,20},{8,24},{12,28},{16,0},{20,4},{24,8},{28,12},{1,17},{... | collective-permute-start | bytes 153608 | tf_op jit(solution)/shard_map/ppermute | solution.py:116
  33.2 6.2 %collective-permute-start.4 = (f32[50,512]{1,0:T(8,128)S(1)}, f32[50,512]{1,0:T(8,128)S(1)}, u32[]{:S(2)}, u32[]{:S(2)}) collective-permute-start(f32[50,512]{1,0:T(8,128)S(1)} %maximum_select_fusion.2), channel_id=1, source_target_pairs={{0,8},{4,12},{8,0},{12,4},{16,24},{20,28},{24,16},{28,20},{1,9},{5... | collective-permute-start | bytes 307208 | tf_op jit(solution)/shard_map/ppermute | solution.py:116
  39.5 6.1 %collective-permute-start.5 = (f32[50,1024]{1,0:T(8,128)S(1)}, f32[50,1024]{1,0:T(8,128)S(1)}, u32[]{:S(2)}, u32[]{:S(2)}) collective-permute-start(f32[50,1024]{1,0:T(8,128)S(1)} %maximum_select_fusion.1), channel_id=1, source_target_pairs={{0,4},{4,0},{8,12},{12,8},{16,20},{20,16},{24,28},{28,24},{1,5},{5... | collective-permute-start | bytes 614408 | tf_op jit(solution)/shard_map/ppermute | solution.py:116
  57.5 5.1 %collective-permute-start.6 = (f32[16,2176]{1,0:T(8,128)S(1)}, f32[16,2176]{1,0:T(8,128)S(1)}, u32[]{:S(2)}, u32[]{:S(2)}) collective-permute-start(f32[16,2176]{1,0:T(8,128)S(1)} %apply_features.4), channel_id=1, source_target_pairs={{0,4},{4,0},{8,12},{12,8},{16,20},{20,16},{24,28},{28,24},{1,5},{5... | collective-permute-start | bytes 417800 | tf_op jit(solution)/shard_map/ppermute | solution.py:116
  62.6 5.1 %collective-permute-start.7 = (f32[16,2176]{1,0:T(8,128)S(1)}, f32[16,2176]{1,0:T(8,128)S(1)}, u32[]{:S(2)}, u32[]{:S(2)}) collective-permute-start(f32[16,2176]{1,0:T(8,128)S(1)} %add.87), channel_id=1, source_target_pairs={{0,8},{4,12},{8,0},{12,4},{16,24},{20,28},{24,16},{28,20},{1,9},{5... | collective-permute-start | bytes 417800 | tf_op jit(solution)/shard_map/ppermute | solution.py:116
  67.8 6.0 %collective-permute-start.8 = (f32[16,2176]{1,0:T(8,128)S(1)}, f32[16,2176]{1,0:T(8,128)S(1)}, u32[]{:S(2)}, u32[]{:S(2)}) collective-permute-start(f32[16,2176]{1,0:T(8,128)S(1)} %add.88), channel_id=1, source_target_pairs={{0,16},{4,20},{8,24},{12,28},{16,0},{20,4},{24,8},{28,12},{1,17},{... | collective-permute-start | bytes 417800 | tf_op jit(solution)/shard_map/ppermute | solution.py:116
  85.0 1.6 collective-permute-start.9
  86.6 8.6 %collective-permute-start.10 = (f32[16,4224]{1,0:T(8,128)S(1)}, f32[16,4224]{1,0:T(8,128)S(1)}, u32[]{:S(2)}, u32[]{:S(2)}) collective-permute-start(f32[16,4224]{1,0:T(8,128)S(1)} %add.90), channel_id=1, source_target_pairs={{0,2},{1,3},{2,0},{3,1},{4,6},{5,7},{6,4},{7,5},{8,10},{9,11},{10,... | collective-permute-start | bytes 811016 | tf_op jit(solution)/shard_map/ppermute | solution.py:116
  106.7 5.1 %collective-permute-start.11 = (f32[16,2176]{1,0:T(8,128)S(1)}, f32[16,2176]{1,0:T(8,128)S(1)}, u32[]{:S(2)}, u32[]{:S(2)}) collective-permute-start(f32[16,2176]{1,0:T(8,128)S(1)} %apply_features.6), channel_id=1, source_target_pairs={{0,4},{4,0},{8,12},{12,8},{16,20},{20,16},{24,28},{28,24},{1,5},{5... | collective-permute-start | bytes 417800 | tf_op jit(solution)/shard_map/ppermute | solution.py:116
  111.8 5.1 %collective-permute-start.12 = (f32[16,2176]{1,0:T(8,128)S(1)}, f32[16,2176]{1,0:T(8,128)S(1)}, u32[]{:S(2)}, u32[]{:S(2)}) collective-permute-start(f32[16,2176]{1,0:T(8,128)S(1)} %add.92), channel_id=1, source_target_pairs={{0,8},{4,12},{8,0},{12,4},{16,24},{20,28},{24,16},{28,20},{1,9},{5... | collective-permute-start | bytes 417800 | tf_op jit(solution)/shard_map/ppermute | solution.py:116
  117.0 6.4 %collective-permute-start.13 = (f32[16,2176]{1,0:T(8,128)S(1)}, f32[16,2176]{1,0:T(8,128)S(1)}, u32[]{:S(2)}, u32[]{:S(2)}) collective-permute-start(f32[16,2176]{1,0:T(8,128)S(1)} %add.93), channel_id=1, source_target_pairs={{0,16},{4,20},{8,24},{12,28},{16,0},{20,4},{24,8},{28,12},{1,17},{... | collective-permute-start | bytes 417800 | tf_op jit(solution)/shard_map/ppermute | solution.py:116
  134.8 1.6 collective-permute-start.14
  136.4 8.6 %collective-permute-start.15 = (f32[16,4224]{1,0:T(8,128)S(1)}, f32[16,4224]{1,0:T(8,128)S(1)}, u32[]{:S(2)}, u32[]{:S(2)}) collective-permute-start(f32[16,4224]{1,0:T(8,128)S(1)} %add.97), channel_id=1, source_target_pairs={{0,2},{1,3},{2,0},{3,1},{4,6},{5,7},{6,4},{7,5},{8,10},{9,11},{10,... | collective-permute-start | bytes 811016 | tf_op jit(solution)/shard_map/ppermute | solution.py:116
  145.4 3.7 %collective-permute-start.16 = (f32[16,128]{1,0:T(8,128)S(1)}, f32[16,128]{1,0:T(8,128)S(1)}, u32[]{:S(2)}, u32[]{:S(2)}) collective-permute-start(f32[16,128]{1,0:T(8,128)S(1)} %broadcast_in_dim.41), channel_id=1, source_target_pairs={{0,4},{4,0},{8,12},{12,8},{16,20},{20,16},{24,28},{28,24},{1,5},{5... | collective-permute-start | bytes 24584 | tf_op jit(solution)/shard_map/ppermute | solution.py:116
  149.1 4.1 %collective-permute-start.17 = (f32[16,128]{1,0:T(8,128)S(1)}, f32[16,128]{1,0:T(8,128)S(1)}, u32[]{:S(2)}, u32[]{:S(2)}) collective-permute-start(f32[16,128]{1,0:T(8,128)S(1)} %broadcast_add_fusion), channel_id=1, source_target_pairs={{0,8},{4,12},{8,0},{12,4},{16,24},{20,28},{24,16},{28,20},{1,9},{5... | collective-permute-start | bytes 24584 | tf_op jit(solution)/shard_map/ppermute | solution.py:116
  153.3 5.1 %collective-permute-start.18 = (f32[16,128]{1,0:T(8,128)S(1)}, f32[16,128]{1,0:T(8,128)S(1)}, u32[]{:S(2)}, u32[]{:S(2)}) collective-permute-start(f32[16,128]{1,0:T(8,128)S(1)} %fusion.17), channel_id=1, source_target_pairs={{0,16},{4,20},{8,24},{12,28},{16,0},{20,4},{24,8},{28,12},{1,17},{... | collective-permute-start | bytes 24584 | tf_op jit(solution)/shard_map/ppermute | solution.py:116

commit v2 on v1

v2 whole, which is shorter than its diff:
```python
import math

import jax
import jax.numpy as jnp
from jax import lax
from jax.experimental import pallas as pl
from jax.experimental.pallas import tpu as pltpu
from jax.sharding import PartitionSpec as P

LAMBDA_REG = 0.01
LOG2E = 1.4426950408889634
DEPTH = 256
BAND = DEPTH // 4
WHOLE = pl.BlockSpec(memory_space=pltpu.VMEM)
BF16, F32 = jnp.bfloat16, jnp.float32


def pieces(x, count):
    out = []
    for unused in range(count):
        part = x.astype(BF16).astype(F32)
        out.append(part)
        x = x - part
    return out


def split(x):
    high = x.astype(BF16)
    return high, (x - high.astype(F32)).astype(BF16)


def augment(ref, x, top, of_path):
    dims, count = x.shape
    rate = 4.0 * LOG2E / dims
    norm = -rate * jnp.sum(x * x, 0, keepdims=True)
    ones = jnp.ones((1, count), F32)
    if of_path:
        high, low = pieces(x * (2.0 * rate), 2)
        bands = (high, high, low, low)
        extra = pieces(norm + top, 3) + [ones] * 3
    else:
        high, low = pieces(x, 2)
        bands = (high, low, high, low)
        extra = [ones] * 3 + pieces(norm, 3)
    ref[...] = jnp.zeros_like(ref)
    for place, band in enumerate(bands):
        ref[place * BAND : place * BAND + dims, :] = band
    for place, row in enumerate(extra):
        ref[dims + place : dims + place + 1, :] = row


def prepare(x, top, of_path, turned):
    count = x.shape[1]
    step = min(512, count)

    def kernel(x_ref, out_ref, full):
        augment(full, x_ref[...], top, of_path)
        for start in range(0, count, step):
            block = full[:, start : start + step]
            if turned:
                out_ref[start : start + step, :] = block.T.astype(BF16)
            else:
                out_ref[:, start : start + step] = block.astype(BF16)

    return pl.pallas_call(
        kernel,
        in_specs=[WHOLE],
        out_specs=WHOLE,
        out_shape=jax.ShapeDtypeStruct((count, DEPTH) if turned else (DEPTH, count), BF16),
        scratch_shapes=[pltpu.VMEM((DEPTH, count), F32)],
        compiler_params=pltpu.CompilerParams(vmem_limit_bytes=12 * 2**20),
        name="prepare",
    )(x)


def gather_block(left, marks, values, top):
    depth, width = left.shape[0], marks.shape[1]
    rows = values.shape[0]
    tile = min(512, depth)
    span = min(1024, width)

    def kernel(left_ref, marks_ref, values_ref, out_ref, full, right):
        augment(full, marks_ref[...], top, False)
        right[...] = full[...].astype(BF16)
        out_ref[...] = jnp.zeros_like(out_ref)

        @pl.loop(0, depth // tile)
        def _(i):
            at = pl.ds(pl.multiple_of(i * tile, tile), tile)
            part_high, part_low = split(values_ref[:, at])
            both = jnp.concatenate([part_high, part_low], 0)
            for start in range(0, width, span):
                to = slice(start, start + span)
                exponent = jnp.dot(left_ref[at, :], right[:, to], preferred_element_type=F32)
                feat = jnp.exp2(jnp.minimum(exponent, top))
                high, low = split(feat)
                first = jnp.dot(both, high, preferred_element_type=F32)
                second = jnp.dot(part_high, low, preferred_element_type=F32)
                out_ref[:, to] += first[:rows] + first[rows:] + second

    return pl.pallas_call(
        kernel,
        in_specs=[WHOLE] * 3,
        out_specs=WHOLE,
        out_shape=jax.ShapeDtypeStruct((rows, width), F32),
        scratch_shapes=[pltpu.VMEM((DEPTH, width), F32), pltpu.VMEM((DEPTH, width), BF16)],
        compiler_params=pltpu.CompilerParams(vmem_limit_bytes=12 * 2**20),
        cost_estimate=pl.CostEstimate(
            flops=4 * depth * width * DEPTH,
            bytes_accessed=4 * depth * DEPTH,
            transcendentals=depth * width,
        ),
        name="gather_block",
    )(left, marks, values)


def pick(state, column):
    dims, count = state.shape
    width = column.shape[1]
    tile = min(512, count)
    span = min(1024, width)

    def kernel(state_ref, column_ref, out_ref, parts, sums):
        parts[...] = jnp.zeros_like(parts)
        for place, piece in enumerate(pieces(state_ref[...], 3)):
            parts[place * BAND : place * BAND + dims, :] = piece.astype(BF16)
        sums[...] = jnp.zeros_like(sums)
        row = lax.broadcasted_iota(jnp.int32, (tile, span), 0)

        @pl.loop(0, count // tile)
        def _(i):
            at = pl.ds(pl.multiple_of(i * tile, tile), tile)
            for start in range(0, width, span):
                to = slice(start, start + span)
                hit = row == column_ref[:, to] - i * tile
                hot = jnp.where(hit, 1.0, 0.0).astype(BF16)
                sums[:, to] += jnp.dot(parts[:, at], hot, preferred_element_type=F32)

        out_ref[...] = (sums[:dims, :] + sums[BAND : BAND + dims, :]) + sums[
            2 * BAND : 2 * BAND + dims, :
        ]

    return pl.pallas_call(
        kernel,
        in_specs=[WHOLE] * 2,
        out_specs=WHOLE,
        out_shape=jax.ShapeDtypeStruct((dims, width), F32),
        scratch_shapes=[
            pltpu.VMEM((3 * BAND, count), BF16),
            pltpu.VMEM((3 * BAND, width), F32),
        ],
        compiler_params=pltpu.CompilerParams(vmem_limit_bytes=12 * 2**20),
        name="pick",
    )(state, column)


def build_features(left, right, top):
    count, width = left.shape[0], right.shape[1]
    tile = min(256, count)

    def kernel(left_ref, right_ref, out_ref):
        @pl.loop(0, count // tile)
        def _(i):
            at = pl.ds(pl.multiple_of(i * tile, tile), tile)
            exponent = jnp.dot(left_ref[at, :], right_ref[...], preferred_element_type=F32)
            feat = jnp.exp2(jnp.minimum(exponent, top))
            high = feat.astype(BF16)
            out_ref[0, at, :] = high
            out_ref[1, at, :] = (feat - high.astype(F32)).astype(BF16)

    return pl.pallas_call(
        kernel,
        in_specs=[WHOLE] * 2,
        out_specs=WHOLE,
        out_shape=pltpu.VMEM((2, count, width), BF16),
        compiler_params=pltpu.CompilerParams(vmem_limit_bytes=8 * 2**20),
        cost_estimate=pl.CostEstimate(
            flops=2 * count * width * DEPTH,
            bytes_accessed=8 * count * width,
            transcendentals=count * width,
        ),
        name="build_features",
    )(left, right)


def spread_half(parts, half, values, other):
    rows = values.shape[0]
    count, width = parts[0].shape[1], parts[0].shape[2] // 2
    tile = min(512, count)

    def kernel(half_ref, values_ref, other_ref, *refs):
        out_ref = refs[-1]
        cols = pl.ds(pl.multiple_of(half_ref[0] * width, width), width)
        v = values_ref[...]
        square = jnp.sum(v * v, 1, keepdims=True)
        mixed = jnp.sum(v * other_ref[...], 1, keepdims=True)
        lane = lax.broadcasted_iota(jnp.int32, (rows, 128), 1)
        out_ref[:, width:] = jnp.where(lane < 64, square, mixed)
        out_ref[:, :width] = jnp.zeros((rows, width), F32)
        for place, part_ref in enumerate(refs[:-1]):
            for start in range(0, count, tile):
                at = slice(start, start + tile)
                high, low = split(values_ref[:, place * count + start : place * count + start + tile])
                both = jnp.concatenate([high, low], 0)
                first = jnp.dot(both, part_ref[0, at, cols], preferred_element_type=F32)
                second = jnp.dot(high, part_ref[1, at, cols], preferred_element_type=F32)
                out_ref[:, :width] += first[:rows] + first[rows:] + second

    return pl.pallas_call(
        kernel,
        in_specs=[pl.BlockSpec(memory_space=pltpu.SMEM)] + [WHOLE] * (2 + len(parts)),
        out_specs=WHOLE,
        out_shape=jax.ShapeDtypeStruct((rows, width + 128), F32),
        compiler_params=pltpu.CompilerParams(vmem_limit_bytes=8 * 2**20),
        name="spread_half",
    )(half, values, other, *parts)


def gather_half(parts, half, values, start_from):
    rows = values.shape[0]
    count, width = parts[0].shape[1], parts[0].shape[2] // 2
    tile = min(512, count)
    lands = count * len(parts)

    def kernel(half_ref, values_ref, from_ref, *refs):
        out_ref = refs[-1]
        cols = pl.ds(pl.multiple_of(half_ref[0] * width, width), width)
        v = values_ref[...]
        out_ref[:, lands:] = from_ref[:, lands:] + jnp.sum(v * v, 1, keepdims=True)
        high, low = split(v)
        both = jnp.concatenate([high, low], 0)
        across = (((1,), (1,)), ((), ()))
        for place, part_ref in enumerate(refs[:-1]):
            for start in range(0, count, tile):
                at = slice(start, start + tile)
                first = lax.dot_general(
                    both, part_ref[0, at, cols], across, preferred_element_type=F32
                )
                second = lax.dot_general(
                    high, part_ref[1, at, cols], across, preferred_element_type=F32
                )
                to = slice(place * count + start, place * count + start + tile)
                out_ref[:, to] = from_ref[:, to] + first[:rows] + first[rows:] + second

    return pl.pallas_call(
        kernel,
        in_specs=[pl.BlockSpec(memory_space=pltpu.SMEM)] + [WHOLE] * (2 + len(parts)),
        out_specs=WHOLE,
        out_shape=jax.ShapeDtypeStruct((rows, lands + 128), F32),
        compiler_params=pltpu.CompilerParams(vmem_limit_bytes=8 * 2**20),
        cost_estimate=pl.CostEstimate(
            flops=2 * lands * width * DEPTH,
            bytes_accessed=4 * lands * width,
            transcendentals=0,
        ),
        name="gather_half",
    )(half, values, start_from, *parts)


def swap(x, axis, bit):
    count = lax.axis_size(axis)
    return lax.ppermute(x, axis, [(i, i ^ bit) for i in range(count)])


def bits(axis):
    out, bit = [], 1
    while bit < lax.axis_size(axis):
        out.append(bit)
        bit *= 2
    return out


def total(x, axis, first=1):
    for bit in bits(axis):
        if bit >= first:
            x = x + swap(x, axis, bit)
    return x


def in_order(upper, own, other):
    return jnp.where(
        upper, jnp.concatenate([other, own], 1), jnp.concatenate([own, other], 1)
    )


def total_by_halves(x, axis, beside):
    here = lax.axis_index(axis)
    for bit in bits(axis):
        half = x.shape[1] // 2
        upper = (here & bit) != 0
        keep = jnp.where(upper, x[:, half:], x[:, :half])
        send = jnp.where(upper, x[:, :half], x[:, half:])
        other = swap(send, axis, bit)
        if bit == 1:
            keep, beside = lax.optimization_barrier((keep, beside))
        x = keep + other
    for bit in reversed(bits(axis)[1:]):
        x = in_order((here & bit) != 0, x, swap(x, axis, bit))
    return x, swap(x, axis, 1), beside


def per_device(state, next_value, brownian, land_index):
    rows = state.shape[1]
    lands = land_index.shape[0]
    half = rows // 2
    paths = rows * lax.axis_size("path")
    landmarks = lands * lax.axis_size("land")
    top = 8.0 * LOG2E - 0.5 * math.log2(landmarks)

    here = lax.axis_index("path")
    core = lax.axis_index("land") & 1
    mine, its = core[None], 1 - core[None]
    picked = pick(state, (land_index - here * rows)[None, :])
    path_right = prepare(state, top, True, False)
    path_left = prepare(state, top, True, True)
    targets = jnp.concatenate([next_value[None, :], next_value[None, :] * brownian], 0)

    marks_own, marks_other, (path_right, path_left, targets) = total_by_halves(
        picked, "path", (path_right, path_left, targets)
    )
    upper = (here & 1) != 0
    sums = [gather_block(path_left, block, targets, top) for block in (marks_own, marks_other)]
    marks = in_order(upper, marks_own, marks_other)
    rhs_part = in_order(upper, *sums)
    marks, rhs_part = lax.optimization_barrier((marks, rhs_part))
    mark_left = prepare(marks, top, False, True)
    chunk = max(lands // 4, 256)
    parts = [
        build_features(mark_left[start : start + chunk], path_right, top)
        for start in range(0, lands, chunk)
    ]
    rhs = total(rhs_part, "path") / paths

    def spread(values, other):
        theirs = spread_half(parts, its, values, other)
        ours = spread_half(parts, mine, values, other)
        ours = total(ours + swap(theirs, "land", 1), "land", 2)
        return ours[:, :half], ours[:, half:]

    first, tail = spread(rhs, rhs)
    norm = tail[:, :1]
    first_other = swap(first, "land", 1)
    back = gather_half(parts, mine, first, jnp.zeros((rhs.shape[0], lands + 128), F32))
    back = total(gather_half(parts, its, first_other, back), "path")
    image = back[:, :lands] / paths + LAMBDA_REG * rhs
    alpha = norm / (back[:, lands : lands + 1] / paths + LAMBDA_REG * norm)
    resid = rhs - alpha * image
    second, tail = spread(resid, rhs)
    norm_next, mixed = tail[:, :1], tail[:, 64:65]
    beta = norm_next / norm
    second_other = swap(second, "land", 1)
    second = second + beta * first
    second_other = second_other + beta * first_other
    squares = jnp.sum(second * second + second_other * second_other, 1, keepdims=True)
    squares = total(jnp.broadcast_to(squares, (rhs.shape[0], 128)), "path")[:, :1]
    length = norm_next + 2.0 * beta * mixed + beta * beta * norm
    alpha_next = norm_next / (squares / paths + LAMBDA_REG * length)
    return in_order(
        core != 0,
        alpha * first + alpha_next * second,
        alpha * first_other + alpha_next * second_other,
    )


def solution(mesh):
    in_specs = (P(None, "path"), P("path"), P(None, "path"), P("land"))
    out_specs = P(None, "path")
    return jax.shard_map(
        per_device, mesh=mesh, in_specs=in_specs, out_specs=out_specs, check_vma=False
    )
```

time: 160 us -> 140 us (0.88)
  starting transfers between devices: 39.2 us -> 26.6 us
  waiting for transfers between devices: 61.9 us -> 53.8 us
  local copies, waits for them, and re-layouts: 7.75 us -> 5.44 us
  Pallas kernels: 46.7 us -> 49 us
    ppermute x19 -> x21, starting transfers between devices: 39.2 us -> 26.6 us  [swap(): return lax.ppermute(x, axis, [(i, i ^ bit) for i in range(count)])]
    ppermute x19 -> x21, waiting for transfers between devices: 61.9 us -> 53.8 us  [swap(): return lax.ppermute(x, axis, [(i, i ^ bit) for i in range(count)])]
    gather x2 -> x0, local copies, waits for them, and re-layouts: 5.82 us -> none  [per_device(): picked = jnp.take(state, land_index % rows, axis=1)]
    unnamed x7 -> x8, local copies, waits for them, and re-layouts: 1.84 us -> 5.27 us
    pallas_call x6 -> x16, Pallas kernels: 46.7 us -> 49 us  [the longest x2 12.6 us: gather_block(): pl.pallas_call(kernel, in_specs=[WHOLE] * 3, out_specs=WHOLE, out_shape=j...]
  transfers between devices with their start and end apart: 19 -> 21, of which waited for: 19 -> 14; matrix products, arithmetic and copies ran while one was open for 0% -> 1% of each run, Pallas kernels for 1% -> 19%
where the time goes in v2:
time: 140 us
  waiting for transfers between devices  53.8 us (38%)
  Pallas kernels  49 us (35%)
  starting transfers between devices  26.6 us (19%)
  local copies, waits for them, and re-layouts  5.44 us (4%)
  other arithmetic  4.55 us (3%)
    ppermute x21, waiting for transfers between devices, swap(): return lax.ppermute(x, axis, [(i, i ^ bit) for i in range(count)])  53.8 us
    ppermute x21, starting transfers between devices, swap(): return lax.ppermute(x, axis, [(i, i ^ bit) for i in range(count)])  26.6 us
    pallas_call x2, Pallas kernels, gather_block(): pl.pallas_call(kernel, in_specs=[WHOLE] * 3, out_specs=WHOLE, out_shape=j...  12.6 us
    pallas_call x4, Pallas kernels, spread_half(): pl.pallas_call(kernel, in_specs=[pl.BlockSpec(memory_space=pltpu.SMEM)] +...  10.3 us
    pallas_call x4, Pallas kernels, build_features(): pl.pallas_call(kernel, in_specs=[WHOLE] * 2, out_specs=WHOLE, out_shape=p...  9.33 us
    pallas_call x2, Pallas kernels, gather_half(): pl.pallas_call(kernel, in_specs=[pl.BlockSpec(memory_space=pltpu.SMEM)] +...  9.28 us
    pallas_call x1, Pallas kernels, pick(): pl.pallas_call(kernel, in_specs=[WHOLE] * 2, out_specs=WHOLE, out_shape=j...  5.41 us
    unnamed x8, local copies, waits for them, and re-layouts  5.27 us
  transfers between devices with their start and end apart: 21, of which 14 were waited for; matrix products, arithmetic and copies ran while one was open for 1% of the time, Pallas kernels for 19%

profile of v2, /device:TPU:0, one launch (start us, length us, event | category | flops | bytes accessed | tf_op | source)
XLA Modules:
  0.0 139.8 jit_solution(11857243750812152426)
XLA Ops:
  1.9 5.4 %pick.1 = f32[50,2048]{1,0:T(8,128)S(1)} custom-call(f32[50,4096]{1,0:T(8,128)S(1)} %copy-done, s32[1,2048]{1,0:T(1,128)S(1)} %bitcast.3), custom_call_target="tpu_custom_call" | custom-call | tf_op jit(solution)/shard_map/pick/pallas_call | solution.py:143
  7.3 3.0 %collective-permute-start = (f32[50,1024]{1,0:T(8,128)S(1)}, f32[50,1024]{1,0:T(8,128)S(1)}, u32[]{:S(2)}, u32[]{:S(2)}) collective-permute-start(f32[50,1024]{1,0:T(8,128)S(1)} %get-tuple-element.21), channel_id=1, source_target_pairs={{0,4},{4,0},{8,12},{12,8},{16,20},{20,16},{24,28},{28,24},{1,5},{5... | collective-permute-start | bytes 614408 | tf_op jit(solution)/shard_map/ppermute | solution.py:262
  18.1 3.2 %collective-permute-done.1 = f32[50,512]{1,0:T(8,128)S(1)} collective-permute-done((f32[50,512]{1,0:T(8,128)S(1)}, f32[50,512]{1,0:T(8,128)S(1)}, u32[]{:S(2)}, u32[]{:S(2)}) %collective-permute-start.1) | collective-permute-done | bytes 102432 | tf_op jit(solution)/shard_map/ppermute | solution.py:262
  21.3 2.7 %collective-permute-start.2 = (f32[50,256]{1,0:T(8,128)S(1)}, f32[50,256]{1,0:T(8,128)S(1)}, u32[]{:S(2)}, u32[]{:S(2)}) collective-permute-start(f32[50,256]{1,0:T(8,128)S(1)} %slice_select_fusion.3), channel_id=1, source_target_pairs={{0,16},{4,20},{8,24},{12,28},{16,0},{20,4},{24,8},{28,12},{1,17},{... | collective-permute-start | bytes 153608 | tf_op jit(solution)/shard_map/ppermute | solution.py:262
  24.0 2.5 %collective-permute-done.2 = f32[50,256]{1,0:T(8,128)S(1)} collective-permute-done((f32[50,256]{1,0:T(8,128)S(1)}, f32[50,256]{1,0:T(8,128)S(1)}, u32[]{:S(2)}, u32[]{:S(2)}) %collective-permute-start.2) | collective-permute-done | bytes 51232 | tf_op jit(solution)/shard_map/ppermute | solution.py:262
  26.5 2.7 %collective-permute-start.3 = (f32[50,256]{1,0:T(8,128)S(1)}, f32[50,256]{1,0:T(8,128)S(1)}, u32[]{:S(2)}, u32[]{:S(2)}) collective-permute-start(f32[50,256]{1,0:T(8,128)S(1)} %select_add_fusion.1), channel_id=1, source_target_pairs={{0,16},{4,20},{8,24},{12,28},{16,0},{20,4},{24,8},{28,12},{1,17},{... | collective-permute-start | bytes 153608 | tf_op jit(solution)/shard_map/ppermute | solution.py:262
  29.2 2.5 %collective-permute-done.3 = f32[50,256]{1,0:T(8,128)S(1)} collective-permute-done((f32[50,256]{1,0:T(8,128)S(1)}, f32[50,256]{1,0:T(8,128)S(1)}, u32[]{:S(2)}, u32[]{:S(2)}) %collective-permute-start.3) | collective-permute-done | bytes 51232 | tf_op jit(solution)/shard_map/ppermute | solution.py:262
  33.5 3.1 %collective-permute-done.4 = f32[50,512]{1,0:T(8,128)S(1)} collective-permute-done((f32[50,512]{1,0:T(8,128)S(1)}, f32[50,512]{1,0:T(8,128)S(1)}, u32[]{:S(2)}, u32[]{:S(2)}) %collective-permute-start.4) | collective-permute-done | bytes 102432 | tf_op jit(solution)/shard_map/ppermute | solution.py:262
  36.6 2.5 %collective-permute-start.5 = (f32[50,1024]{1,0:T(8,128)S(1)}, f32[50,1024]{1,0:T(8,128)S(1)}, u32[]{:S(2)}, u32[]{:S(2)}) collective-permute-start(f32[50,1024]{1,0:T(8,128)S(1)} %maximum_select_fusion.2.marks_ref), channel_id=1, source_target_pairs={{0,4},{4,0},{8,12},{12,8},{16,20},{20,16},{24,28},{28,24},{1,5},{5... | collective-permute-start | bytes 614408 | tf_op jit(solution)/shard_map/ppermute | solution.py:262
  40.8 6.3 %gather_block.3 = f32[16,1024]{1,0:T(8,128)S(1)} custom-call(bf16[4096,256]{1,0:T(8,128)(2,1)S(1)} %copy-done.3, f32[50,1024]{1,0:T(8,128)S(1)} %maximum_select_fusion.2.marks_ref, f32[16,4096]{1,0:T(8,128)S(1)} %pad_maximum_fusion.values_ref), custom_call_target="tpu_custom_call" | custom-call | flops 4294967296 | bytes 4194304 | tf_op jit(solution)/shard_map/gather_block/pallas_call | solution.py:101
  47.0 6.3 %gather_block.2 = f32[16,1024]{1,0:T(8,128)S(1)} custom-call(bf16[4096,256]{1,0:T(8,128)(2,1)S(1)} %copy-done.3, f32[50,1024]{1,0:T(8,128)S(1)} %collective-permute-done.5.marks_ref, f32[16,4096]{1,0:T(8,128)S(1)} %pad_maximum_fusion.values_ref), custom_call_target="tpu_custom_call" | custom-call | flops 4294967296 | bytes 4194304 | tf_op jit(solution)/shard_map/gather_block/pallas_call | solution.py:101
  54.0 4.9 %collective-permute-done.6 = f32[16,2048]{1,0:T(8,128)S(1)} collective-permute-done((f32[16,2048]{1,0:T(8,128)S(1)}, f32[16,2048]{1,0:T(8,128)S(1)}, u32[]{:S(2)}, u32[]{:S(2)}) %collective-permute-start.6) | collective-permute-done | bytes 131104 | tf_op jit(solution)/shard_map/ppermute | solution.py:262
  58.8 2.1 %collective-permute-start.7 = (f32[16,2048]{1,0:T(8,128)S(1)}, f32[16,2048]{1,0:T(8,128)S(1)}, u32[]{:S(2)}, u32[]{:S(2)}) collective-permute-start(f32[16,2048]{1,0:T(8,128)S(1)} %add.81), channel_id=1, source_target_pairs={{0,8},{4,12},{8,0},{12,4},{16,24},{20,28},{24,16},{28,20},{1,9},{5... | collective-permute-start | bytes 393224 | tf_op jit(solution)/shard_map/ppermute | solution.py:262
  60.9 2.3 %build_features.5.refs_1_ = bf16[2,512,4096]{2,1,0:T(8,128)(2,1)S(1)} custom-call(bf16[512,256]{1,0:T(8,128)(2,1)S(1)} %get-tuple-element.19.left_ref, bf16[256,4096]{1,0:T(8,128)(2,1)S(1)} %prepare.3.right_ref), custom_call_target="tpu_custom_call" | custom-call | flops 1073741824 | bytes 16777216 | tf_op jit(solution)/shard_map/build_features/pallas_call | solution.py:171
  63.2 2.3 %build_features.6.refs_2_ = bf16[2,512,4096]{2,1,0:T(8,128)(2,1)S(1)} custom-call(bf16[512,256]{1,0:T(8,128)(2,1)S(1)} %get-tuple-element.18.left_ref, bf16[256,4096]{1,0:T(8,128)(2,1)S(1)} %prepare.3.right_ref), custom_call_target="tpu_custom_call" | custom-call | flops 1073741824 | bytes 16777216 | tf_op jit(solution)/shard_map/build_features/pallas_call | solution.py:171
  65.6 2.4 %collective-permute-start.8 = (f32[16,2048]{1,0:T(8,128)S(1)}, f32[16,2048]{1,0:T(8,128)S(1)}, u32[]{:S(2)}, u32[]{:S(2)}) collective-permute-start(f32[16,2048]{1,0:T(8,128)S(1)} %add.82), channel_id=1, source_target_pairs={{0,16},{4,20},{8,24},{12,28},{16,0},{20,4},{24,8},{28,12},{1,17},{... | collective-permute-start | bytes 393224 | tf_op jit(solution)/shard_map/ppermute | solution.py:262
  68.0 2.3 %build_features.7.refs_3_ = bf16[2,512,4096]{2,1,0:T(8,128)(2,1)S(1)} custom-call(bf16[512,256]{1,0:T(8,128)(2,1)S(1)} %get-tuple-element.17.left_ref, bf16[256,4096]{1,0:T(8,128)(2,1)S(1)} %prepare.3.right_ref), custom_call_target="tpu_custom_call" | custom-call | flops 1073741824 | bytes 16777216 | tf_op jit(solution)/shard_map/build_features/pallas_call | solution.py:171
  70.3 2.5 %build_features.4.refs_0_ = bf16[2,512,4096]{2,1,0:T(8,128)(2,1)S(1)} custom-call(bf16[512,256]{1,0:T(8,128)(2,1)S(1)} %get-tuple-element.20.left_ref, bf16[256,4096]{1,0:T(8,128)(2,1)S(1)} %prepare.3.right_ref), custom_call_target="tpu_custom_call" | custom-call | flops 1073741824 | bytes 16777216 | tf_op jit(solution)/shard_map/build_features/pallas_call | solution.py:171
  72.8 2.5 %spread_half.5 = f32[16,2176]{1,0:T(8,128)S(1)} custom-call(s32[1]{0:T(128)S(6)} %sub.14.half_ref, f32[16,2048]{1,0:T(8,128)S(1)} %broadcast_multiply_fusion.1.values_ref.other_ref, f32[16,2048]{1,0:T(8,128)S(1)} %broadcast_multiply_fusion.1.values_ref.other_ref, bf16[2,512,4096]{2,1,0:T(8,128)(2,1)S(1)} %build_features.4.refs_0_, ...), custom_call_target="tpu_custom_call" | custom-call | tf_op jit(solution)/shard_map/spread_half/pallas_call | solution.py:209
  75.3 2.5 %spread_half.4 = f32[16,2176]{1,0:T(8,128)S(1)} custom-call(s32[1]{0:T(128)} %bitcast.half_ref, f32[16,2048]{1,0:T(8,128)S(1)} %broadcast_multiply_fusion.1.values_ref.other_ref, f32[16,2048]{1,0:T(8,128)S(1)} %broadcast_multiply_fusion.1.values_ref.other_ref, bf16[2,512,4096]{2,1,0:T(8,128)(2,1)S(1)} %build_features.4.refs_0_, ...), custom_call_target="tpu_custom_call" | custom-call | tf_op jit(solution)/shard_map/spread_half/pallas_call | solution.py:209
  79.4 4.6 %collective-permute-done.10 = f32[16,2176]{1,0:T(8,128)S(1)} collective-permute-done((f32[16,2176]{1,0:T(8,128)S(1)}, f32[16,2176]{1,0:T(8,128)S(1)}, u32[]{:S(2)}, u32[]{:S(2)}) %collective-permute-start.10) | collective-permute-done | bytes 139296 | tf_op jit(solution)/shard_map/ppermute | solution.py:262
  84.2 4.6 %gather_half.2.from_ref = f32[16,2176]{1,0:T(8,128)S(1)} custom-call(s32[1]{0:T(128)} %bitcast.half_ref, f32[16,2048]{1,0:T(8,128)S(1)} %slice.94.values_ref, f32[16,2176]{1,0:T(8,128)S(1)} %broadcast_in_dim.23.from_ref, bf16[2,512,4096]{2,1,0:T(8,128)(2,1)S(1)} %build_features.4.refs_0_, bf16[2,512,4096]{2,1,0:T(8,128)(2,1)S(1)} %build_features.5.refs_1_, ...), custom_call_target="tpu_custom_call" | custom-call | flops 2147483648 | bytes 16777216 | tf_op jit(solution)/shard_map/gather_half/pallas_call | solution.py:245
  88.8 4.6 %gather_half.3 = f32[16,2176]{1,0:T(8,128)S(1)} custom-call(s32[1]{0:T(128)S(6)} %sub.14.half_ref, f32[16,2048]{1,0:T(8,128)S(1)} %collective-permute-done.11.values_ref, f32[16,2176]{1,0:T(8,128)S(1)} %gather_half.2.from_ref, bf16[2,512,4096]{2,1,0:T(8,128)(2,1)S(1)} %build_features.4.refs_0_, bf16[2,512,4096]{2,1,0:T(8,128)(2,1)S(1)} %build_features.5.refs_1_, ...), custom_call_target="tpu_custom_call" | custom-call | flops 2147483648 | bytes 16777216 | tf_op jit(solution)/shard_map/gather_half/pallas_call | solution.py:245
  93.6 5.9 %collective-permute-done.12 = f32[16,2176]{1,0:T(8,128)S(1)} collective-permute-done((f32[16,2176]{1,0:T(8,128)S(1)}, f32[16,2176]{1,0:T(8,128)S(1)}, u32[]{:S(2)}, u32[]{:S(2)}) %collective-permute-start.12) | collective-permute-done | bytes 139296 | tf_op jit(solution)/shard_map/ppermute | solution.py:262
  100.4 4.5 %collective-permute-done.13 = f32[16,2176]{1,0:T(8,128)S(1)} collective-permute-done((f32[16,2176]{1,0:T(8,128)S(1)}, f32[16,2176]{1,0:T(8,128)S(1)}, u32[]{:S(2)}, u32[]{:S(2)}) %collective-permute-start.13) | collective-permute-done | bytes 139296 | tf_op jit(solution)/shard_map/ppermute | solution.py:262
  106.6 6.7 %collective-permute-done.14 = f32[16,2176]{1,0:T(8,128)S(1)} collective-permute-done((f32[16,2176]{1,0:T(8,128)S(1)}, f32[16,2176]{1,0:T(8,128)S(1)}, u32[]{:S(2)}, u32[]{:S(2)}) %collective-permute-start.14) | collective-permute-done | bytes 139296 | tf_op jit(solution)/shard_map/ppermute | solution.py:262
  113.5 2.7 %spread_half.7 = f32[16,2176]{1,0:T(8,128)S(1)} custom-call(s32[1]{0:T(128)S(6)} %sub.14.half_ref, f32[16,2048]{1,0:T(8,128)S(1)} %fusion.2.values_ref, f32[16,2048]{1,0:T(8,128)S(1)} %broadcast_multiply_fusion.1.values_ref.other_ref, bf16[2,512,4096]{2,1,0:T(8,128)(2,1)S(1)} %build_features.4.refs_0_, bf16[2,512,4096]{2,1,0:T(8,128)(2,1)S(1)} %build_features.5.refs_1_, ...), custom_call_target="tpu_custom_call" | custom-call | tf_op jit(solution)/shard_map/spread_half/pallas_call | solution.py:209
  116.3 2.5 %spread_half.6 = f32[16,2176]{1,0:T(8,128)S(1)} custom-call(s32[1]{0:T(128)} %bitcast.half_ref, f32[16,2048]{1,0:T(8,128)S(1)} %fusion.2.values_ref, f32[16,2048]{1,0:T(8,128)S(1)} %broadcast_multiply_fusion.1.values_ref.other_ref, bf16[2,512,4096]{2,1,0:T(8,128)(2,1)S(1)} %build_features.4.refs_0_, bf16[2,512,4096]{2,1,0:T(8,128)(2,1)S(1)} %build_features.5.refs_1_, ...), custom_call_target="tpu_custom_call" | custom-call | tf_op jit(solution)/shard_map/spread_half/pallas_call | solution.py:209
  120.4 4.6 %collective-permute-done.16 = f32[16,2176]{1,0:T(8,128)S(1)} collective-permute-done((f32[16,2176]{1,0:T(8,128)S(1)}, f32[16,2176]{1,0:T(8,128)S(1)}, u32[]{:S(2)}, u32[]{:S(2)}) %collective-permute-start.16) | collective-permute-done | bytes 139296 | tf_op jit(solution)/shard_map/ppermute | solution.py:262
  127.3 3.1 %collective-permute-done.18 = f32[16,128]{1,0:T(8,128)S(1)} collective-permute-done((f32[16,128]{1,0:T(8,128)S(1)}, f32[16,128]{1,0:T(8,128)S(1)}, u32[]{:S(2)}, u32[]{:S(2)}) %collective-permute-start.18) | collective-permute-done | bytes 8224 | tf_op jit(solution)/shard_map/ppermute | solution.py:262
  130.4 3.6 %collective-permute-done.19 = f32[16,128]{1,0:T(8,128)S(1)} collective-permute-done((f32[16,128]{1,0:T(8,128)S(1)}, f32[16,128]{1,0:T(8,128)S(1)}, u32[]{:S(2)}, u32[]{:S(2)}) %collective-permute-start.19) | collective-permute-done | bytes 8224 | tf_op jit(solution)/shard_map/ppermute | solution.py:262
  135.4 3.3 %collective-permute-done.20 = f32[16,128]{1,0:T(8,128)S(1)} collective-permute-done((f32[16,128]{1,0:T(8,128)S(1)}, f32[16,128]{1,0:T(8,128)S(1)}, u32[]{:S(2)}, u32[]{:S(2)}) %collective-permute-start.20) | collective-permute-done | bytes 8224 | tf_op jit(solution)/shard_map/ppermute | solution.py:262
  (71 shorter events, 24.5 us)
Async XLA Ops:
  0.7 1.2 copy-start
  7.3 9.0 %collective-permute-start = (f32[50,1024]{1,0:T(8,128)S(1)}, f32[50,1024]{1,0:T(8,128)S(1)}, u32[]{:S(2)}, u32[]{:S(2)}) collective-permute-start(f32[50,1024]{1,0:T(8,128)S(1)} %get-tuple-element.21), channel_id=1, source_target_pairs={{0,4},{4,0},{8,12},{12,8},{16,20},{20,16},{24,28},{28,24},{1,5},{5... | collective-permute-start | bytes 614408 | tf_op jit(solution)/shard_map/ppermute | solution.py:262
  12.1 1.2 copy-start.1
  15.0 1.3 copy-start.2
  16.4 4.9 %collective-permute-start.1 = (f32[50,512]{1,0:T(8,128)S(1)}, f32[50,512]{1,0:T(8,128)S(1)}, u32[]{:S(2)}, u32[]{:S(2)}) collective-permute-start(f32[50,512]{1,0:T(8,128)S(1)} %slice_select_fusion.2), channel_id=1, source_target_pairs={{0,8},{4,12},{8,0},{12,4},{16,24},{20,28},{24,16},{28,20},{1,9},{5... | collective-permute-start | bytes 307208 | tf_op jit(solution)/shard_map/ppermute | solution.py:262
  21.3 5.1 %collective-permute-start.2 = (f32[50,256]{1,0:T(8,128)S(1)}, f32[50,256]{1,0:T(8,128)S(1)}, u32[]{:S(2)}, u32[]{:S(2)}) collective-permute-start(f32[50,256]{1,0:T(8,128)S(1)} %slice_select_fusion.3), channel_id=1, source_target_pairs={{0,16},{4,20},{8,24},{12,28},{16,0},{20,4},{24,8},{28,12},{1,17},{... | collective-permute-start | bytes 153608 | tf_op jit(solution)/shard_map/ppermute | solution.py:262
  26.5 5.2 %collective-permute-start.3 = (f32[50,256]{1,0:T(8,128)S(1)}, f32[50,256]{1,0:T(8,128)S(1)}, u32[]{:S(2)}, u32[]{:S(2)}) collective-permute-start(f32[50,256]{1,0:T(8,128)S(1)} %select_add_fusion.1), channel_id=1, source_target_pairs={{0,16},{4,20},{8,24},{12,28},{16,0},{20,4},{24,8},{28,12},{1,17},{... | collective-permute-start | bytes 153608 | tf_op jit(solution)/shard_map/ppermute | solution.py:262
  31.8 4.9 %collective-permute-start.4 = (f32[50,512]{1,0:T(8,128)S(1)}, f32[50,512]{1,0:T(8,128)S(1)}, u32[]{:S(2)}, u32[]{:S(2)}) collective-permute-start(f32[50,512]{1,0:T(8,128)S(1)} %maximum_select_fusion.4), channel_id=1, source_target_pairs={{0,8},{4,12},{8,0},{12,4},{16,24},{20,28},{24,16},{28,20},{1,9},{5... | collective-permute-start | bytes 307208 | tf_op jit(solution)/shard_map/ppermute | solution.py:262
  36.6 10.4 %collective-permute-start.5 = (f32[50,1024]{1,0:T(8,128)S(1)}, f32[50,1024]{1,0:T(8,128)S(1)}, u32[]{:S(2)}, u32[]{:S(2)}) collective-permute-start(f32[50,1024]{1,0:T(8,128)S(1)} %maximum_select_fusion.2.marks_ref), channel_id=1, source_target_pairs={{0,4},{4,0},{8,12},{12,8},{16,20},{20,16},{24,28},{28,24},{1,5},{5... | collective-permute-start | bytes 614408 | tf_op jit(solution)/shard_map/ppermute | solution.py:262
  39.2 1.6 %copy-start.3 = (bf16[4096,256]{1,0:T(8,128)(2,1)S(1)}, bf16[4096,256]{1,0:T(8,128)(2,1)}, u32[]{:S(2)}) copy-start(bf16[4096,256]{1,0:T(8,128)(2,1)} %copy-done.2) | copy-start | bytes 6291460
  53.8 5.0 %collective-permute-start.6 = (f32[16,2048]{1,0:T(8,128)S(1)}, f32[16,2048]{1,0:T(8,128)S(1)}, u32[]{:S(2)}, u32[]{:S(2)}) collective-permute-start(f32[16,2048]{1,0:T(8,128)S(1)} %maximum_select_fusion.3), channel_id=1, source_target_pairs={{0,4},{4,0},{8,12},{12,8},{16,20},{20,16},{24,28},{28,24},{1,5},{5... | collective-permute-start | bytes 393224 | tf_op jit(solution)/shard_map/ppermute | solution.py:262
  58.8 6.7 %collective-permute-start.7 = (f32[16,2048]{1,0:T(8,128)S(1)}, f32[16,2048]{1,0:T(8,128)S(1)}, u32[]{:S(2)}, u32[]{:S(2)}) collective-permute-start(f32[16,2048]{1,0:T(8,128)S(1)} %add.81), channel_id=1, source_target_pairs={{0,8},{4,12},{8,0},{12,4},{16,24},{20,28},{24,16},{28,20},{1,9},{5... | collective-permute-start | bytes 393224 | tf_op jit(solution)/shard_map/ppermute | solution.py:262
  65.6 7.2 %collective-permute-start.8 = (f32[16,2048]{1,0:T(8,128)S(1)}, f32[16,2048]{1,0:T(8,128)S(1)}, u32[]{:S(2)}, u32[]{:S(2)}) collective-permute-start(f32[16,2048]{1,0:T(8,128)S(1)} %add.82), channel_id=1, source_target_pairs={{0,16},{4,20},{8,24},{12,28},{16,0},{20,4},{24,8},{28,12},{1,17},{... | collective-permute-start | bytes 393224 | tf_op jit(solution)/shard_map/ppermute | solution.py:262
  75.3 2.5 %collective-permute-start.9 = (f32[16,2176]{1,0:T(8,128)S(1)}, f32[16,2176]{1,0:T(8,128)S(1)}, u32[]{:S(2)}, u32[]{:S(2)}) collective-permute-start(f32[16,2176]{1,0:T(8,128)S(1)} %spread_half.5), channel_id=1, source_target_pairs={{0,1},{1,0},{2,3},{3,2},{4,5},{5,4},{6,7},{7,6},{8,9},{9,8},{10,11... | collective-permute-start | bytes 417800 | tf_op jit(solution)/shard_map/ppermute | solution.py:262
  77.9 6.1 %collective-permute-start.10 = (f32[16,2176]{1,0:T(8,128)S(1)}, f32[16,2176]{1,0:T(8,128)S(1)}, u32[]{:S(2)}, u32[]{:S(2)}) collective-permute-start(f32[16,2176]{1,0:T(8,128)S(1)} %add.84), channel_id=1, source_target_pairs={{0,2},{1,3},{2,0},{3,1},{4,6},{5,7},{6,4},{7,5},{8,10},{9,11},{10,... | collective-permute-start | bytes 417800 | tf_op jit(solution)/shard_map/ppermute | solution.py:262
  84.1 4.7 %collective-permute-start.11 = (f32[16,2048]{1,0:T(8,128)S(1)}, f32[16,2048]{1,0:T(8,128)S(1)}, u32[]{:S(2)}, u32[]{:S(2)}) collective-permute-start(f32[16,2048]{1,0:T(8,128)S(1)} %slice.94.values_ref), channel_id=1, source_target_pairs={{0,1},{1,0},{2,3},{3,2},{4,5},{5,4},{6,7},{7,6},{8,9},{9,8},{10,11... | collective-permute-start | bytes 393224 | tf_op jit(solution)/shard_map/ppermute | solution.py:262
  93.5 6.1 %collective-permute-start.12 = (f32[16,2176]{1,0:T(8,128)S(1)}, f32[16,2176]{1,0:T(8,128)S(1)}, u32[]{:S(2)}, u32[]{:S(2)}) collective-permute-start(f32[16,2176]{1,0:T(8,128)S(1)} %gather_half.3), channel_id=1, source_target_pairs={{0,4},{4,0},{8,12},{12,8},{16,20},{20,16},{24,28},{28,24},{1,5},{5... | collective-permute-start | bytes 417800 | tf_op jit(solution)/shard_map/ppermute | solution.py:262
  99.6 5.4 %collective-permute-start.13 = (f32[16,2176]{1,0:T(8,128)S(1)}, f32[16,2176]{1,0:T(8,128)S(1)}, u32[]{:S(2)}, u32[]{:S(2)}) collective-permute-start(f32[16,2176]{1,0:T(8,128)S(1)} %add.86), channel_id=1, source_target_pairs={{0,8},{4,12},{8,0},{12,4},{16,24},{20,28},{24,16},{28,20},{1,9},{5... | collective-permute-start | bytes 417800 | tf_op jit(solution)/shard_map/ppermute | solution.py:262
  104.9 8.3 %collective-permute-start.14 = (f32[16,2176]{1,0:T(8,128)S(1)}, f32[16,2176]{1,0:T(8,128)S(1)}, u32[]{:S(2)}, u32[]{:S(2)}) collective-permute-start(f32[16,2176]{1,0:T(8,128)S(1)} %add.87), channel_id=1, source_target_pairs={{0,16},{4,20},{8,24},{12,28},{16,0},{20,4},{24,8},{28,12},{1,17},{... | collective-permute-start | bytes 417800 | tf_op jit(solution)/shard_map/ppermute | solution.py:262
  116.3 2.5 %collective-permute-start.15 = (f32[16,2176]{1,0:T(8,128)S(1)}, f32[16,2176]{1,0:T(8,128)S(1)}, u32[]{:S(2)}, u32[]{:S(2)}) collective-permute-start(f32[16,2176]{1,0:T(8,128)S(1)} %spread_half.7), channel_id=1, source_target_pairs={{0,1},{1,0},{2,3},{3,2},{4,5},{5,4},{6,7},{7,6},{8,9},{9,8},{10,11... | collective-permute-start | bytes 417800 | tf_op jit(solution)/shard_map/ppermute | solution.py:262
  118.8 6.1 %collective-permute-start.16 = (f32[16,2176]{1,0:T(8,128)S(1)}, f32[16,2176]{1,0:T(8,128)S(1)}, u32[]{:S(2)}, u32[]{:S(2)}) collective-permute-start(f32[16,2176]{1,0:T(8,128)S(1)} %add.91), channel_id=1, source_target_pairs={{0,2},{1,3},{2,0},{3,1},{4,6},{5,7},{6,4},{7,5},{8,10},{9,11},{10,... | collective-permute-start | bytes 417800 | tf_op jit(solution)/shard_map/ppermute | solution.py:262
  125.0 1.4 %collective-permute-start.17 = (f32[16,2048]{1,0:T(8,128)S(1)}, f32[16,2048]{1,0:T(8,128)S(1)}, u32[]{:S(2)}, u32[]{:S(2)}) collective-permute-start(f32[16,2048]{1,0:T(8,128)S(1)} %slice.98), channel_id=1, source_target_pairs={{0,1},{1,0},{2,3},{3,2},{4,5},{5,4},{6,7},{7,6},{8,9},{9,8},{10,11... | collective-permute-start | bytes 393224 | tf_op jit(solution)/shard_map/ppermute | solution.py:262
  126.7 3.7 %collective-permute-start.18 = (f32[16,128]{1,0:T(8,128)S(1)}, f32[16,128]{1,0:T(8,128)S(1)}, u32[]{:S(2)}, u32[]{:S(2)}) collective-permute-start(f32[16,128]{1,0:T(8,128)S(1)} %broadcast_in_dim.24), channel_id=1, source_target_pairs={{0,4},{4,0},{8,12},{12,8},{16,20},{20,16},{24,28},{28,24},{1,5},{5... | collective-permute-start | bytes 24584 | tf_op jit(solution)/shard_map/ppermute | solution.py:262
  130.4 3.7 %collective-permute-start.19 = (f32[16,128]{1,0:T(8,128)S(1)}, f32[16,128]{1,0:T(8,128)S(1)}, u32[]{:S(2)}, u32[]{:S(2)}) collective-permute-start(f32[16,128]{1,0:T(8,128)S(1)} %broadcast_add_fusion), channel_id=1, source_target_pairs={{0,8},{4,12},{8,0},{12,4},{16,24},{20,28},{24,16},{28,20},{1,9},{5... | collective-permute-start | bytes 24584 | tf_op jit(solution)/shard_map/ppermute | solution.py:262
  134.2 4.6 %collective-permute-start.20 = (f32[16,128]{1,0:T(8,128)S(1)}, f32[16,128]{1,0:T(8,128)S(1)}, u32[]{:S(2)}, u32[]{:S(2)}) collective-permute-start(f32[16,128]{1,0:T(8,128)S(1)} %fusion.15), channel_id=1, source_target_pairs={{0,16},{4,20},{8,24},{12,28},{16,0},{20,4},{24,8},{28,12},{1,17},{... | collective-permute-start | bytes 24584 | tf_op jit(solution)/shard_map/ppermute | solution.py:262

commit v3 on v2

--- a/solution.py
+++ b/solution.py
@@ -9,8 +9,8 @@
 
 LAMBDA_REG = 0.01
 LOG2E = 1.4426950408889634
-DEPTH = 256
-BAND = DEPTH // 4
+BAND = 64
+DEPTH = 6 * BAND
 WHOLE = pl.BlockSpec(memory_space=pltpu.VMEM)
 BF16, F32 = jnp.bfloat16, jnp.float32
 
@@ -29,89 +29,96 @@
     return high, (x - high.astype(F32)).astype(BF16)
 
 
-def augment(ref, x, top, of_path):
-    dims, count = x.shape
-    rate = 4.0 * LOG2E / dims
-    norm = -rate * jnp.sum(x * x, 0, keepdims=True)
-    ones = jnp.ones((1, count), F32)
+def split_rows(x):
+    return jnp.concatenate([part.astype(BF16) for part in pieces(x, 3)], 0)
+
+
+def add_rows(first, second, rows):
+    small = first[2 * rows :] + (second[:rows] + second[rows:])
+    return first[:rows] + (first[rows : 2 * rows] + small)
+
+
+def rate_of(x):
+    return 4.0 * LOG2E / x.shape[0]
+
+
+def augment(ref, x, of_path):
+    dims = x.shape[0]
     if of_path:
-        high, low = pieces(x * (2.0 * rate), 2)
-        bands = (high, high, low, low)
-        extra = pieces(norm + top, 3) + [ones] * 3
+        high, middle, low = pieces(x * (2.0 * rate_of(x)), 3)
+        bands = (high, high, middle, high, middle, low)
     else:
-        high, low = pieces(x, 2)
-        bands = (high, low, high, low)
-        extra = [ones] * 3 + pieces(norm, 3)
+        high, middle, low = pieces(x, 3)
+        bands = (high, middle, high, low, middle, high)
     ref[...] = jnp.zeros_like(ref)
     for place, band in enumerate(bands):
         ref[place * BAND : place * BAND + dims, :] = band
-    for place, row in enumerate(extra):
-        ref[dims + place : dims + place + 1, :] = row
-
-
-def prepare(x, top, of_path, turned):
+
+
+def prepare(x):
     count = x.shape[1]
-    step = min(512, count)
 
     def kernel(x_ref, out_ref, full):
-        augment(full, x_ref[...], top, of_path)
-        for start in range(0, count, step):
-            block = full[:, start : start + step]
-            if turned:
-                out_ref[start : start + step, :] = block.T.astype(BF16)
-            else:
-                out_ref[:, start : start + step] = block.astype(BF16)
+        augment(full, x_ref[...], True)
+        out_ref[...] = full[...].astype(BF16)
 
     return pl.pallas_call(
         kernel,
         in_specs=[WHOLE],
         out_specs=WHOLE,
-        out_shape=jax.ShapeDtypeStruct((count, DEPTH) if turned else (DEPTH, count), BF16),
+        out_shape=jax.ShapeDtypeStruct((DEPTH, count), BF16),
         scratch_shapes=[pltpu.VMEM((DEPTH, count), F32)],
-        compiler_params=pltpu.CompilerParams(vmem_limit_bytes=12 * 2**20),
+        cost_estimate=pl.CostEstimate(
+            flops=0, bytes_accessed=4 * count * DEPTH, transcendentals=0
+        ),
+        compiler_params=pltpu.CompilerParams(vmem_limit_bytes=8 * 2**20),
         name="prepare",
     )(x)
 
 
-def gather_block(left, marks, values, top):
-    depth, width = left.shape[0], marks.shape[1]
+def gather_block(paths, norm, marks, values, top):
+    depth, width = paths.shape[1], marks.shape[1]
     rows = values.shape[0]
     tile = min(512, depth)
     span = min(1024, width)
 
-    def kernel(left_ref, marks_ref, values_ref, out_ref, full, right):
-        augment(full, marks_ref[...], top, False)
+    def kernel(paths_ref, norm_ref, marks_ref, values_ref, out_ref, full, right):
+        m = marks_ref[...]
+        augment(full, m, False)
+        mark_norm = -rate_of(m) * jnp.sum(m * m, 0, keepdims=True)
         right[...] = full[...].astype(BF16)
         out_ref[...] = jnp.zeros_like(out_ref)
 
         @pl.loop(0, depth // tile)
         def _(i):
             at = pl.ds(pl.multiple_of(i * tile, tile), tile)
-            part_high, part_low = split(values_ref[:, at])
-            both = jnp.concatenate([part_high, part_low], 0)
+            left = paths_ref[:, at].astype(F32).T.astype(BF16)
+            norms = norm_ref[:, at].T[:, :1]
+            left_rows = split_rows(values_ref[:, at])
             for start in range(0, width, span):
                 to = slice(start, start + span)
-                exponent = jnp.dot(left_ref[at, :], right[:, to], preferred_element_type=F32)
+                exponent = jnp.dot(left, right[:, to], preferred_element_type=F32)
+                exponent = exponent + (norms + mark_norm[:, to])
                 feat = jnp.exp2(jnp.minimum(exponent, top))
                 high, low = split(feat)
-                first = jnp.dot(both, high, preferred_element_type=F32)
-                second = jnp.dot(part_high, low, preferred_element_type=F32)
-                out_ref[:, to] += first[:rows] + first[rows:] + second
-
-    return pl.pallas_call(
-        kernel,
-        in_specs=[WHOLE] * 3,
+                first = jnp.dot(left_rows, high, preferred_element_type=F32)
+                second = jnp.dot(left_rows[: 2 * rows], low, preferred_element_type=F32)
+                out_ref[:, to] += add_rows(first, second, rows)
+
+    return pl.pallas_call(
+        kernel,
+        in_specs=[WHOLE] * 4,
         out_specs=WHOLE,
         out_shape=jax.ShapeDtypeStruct((rows, width), F32),
         scratch_shapes=[pltpu.VMEM((DEPTH, width), F32), pltpu.VMEM((DEPTH, width), BF16)],
-        compiler_params=pltpu.CompilerParams(vmem_limit_bytes=12 * 2**20),
+        compiler_params=pltpu.CompilerParams(vmem_limit_bytes=8 * 2**20),
         cost_estimate=pl.CostEstimate(
             flops=4 * depth * width * DEPTH,
             bytes_accessed=4 * depth * DEPTH,
             transcendentals=depth * width,
         ),
         name="gather_block",
-    )(left, marks, values)
+    )(paths, norm, marks, values)
 
 
 def pick(state, column):
@@ -149,30 +156,42 @@
             pltpu.VMEM((3 * BAND, count), BF16),
             pltpu.VMEM((3 * BAND, width), F32),
         ],
-        compiler_params=pltpu.CompilerParams(vmem_limit_bytes=12 * 2**20),
+        compiler_params=pltpu.CompilerParams(vmem_limit_bytes=8 * 2**20),
         name="pick",
     )(state, column)
 
 
-def build_features(left, right, top):
-    count, width = left.shape[0], right.shape[1]
+def build_features(marks, right, norm, top):
+    count, width = marks.shape[1], right.shape[1]
     tile = min(256, count)
 
-    def kernel(left_ref, right_ref, out_ref):
+    def kernel(marks_ref, right_ref, norm_ref, out_ref, full, left, norms):
+        m = marks_ref[...]
+        augment(full, m, False)
+        mark_norm = -rate_of(m) * jnp.sum(m * m, 0, keepdims=True)
+        norms[...] = jnp.broadcast_to(mark_norm, (8, count)).T
+        left[...] = full[...].T.astype(BF16)
+
         @pl.loop(0, count // tile)
         def _(i):
             at = pl.ds(pl.multiple_of(i * tile, tile), tile)
-            exponent = jnp.dot(left_ref[at, :], right_ref[...], preferred_element_type=F32)
+            exponent = jnp.dot(left[at, :], right_ref[...], preferred_element_type=F32)
+            exponent = exponent + (norms[at, :1] + norm_ref[:1, :])
             feat = jnp.exp2(jnp.minimum(exponent, top))
-            high = feat.astype(BF16)
+            high, low = split(feat)
             out_ref[0, at, :] = high
-            out_ref[1, at, :] = (feat - high.astype(F32)).astype(BF16)
-
-    return pl.pallas_call(
-        kernel,
-        in_specs=[WHOLE] * 2,
+            out_ref[1, at, :] = low
+
+    return pl.pallas_call(
+        kernel,
+        in_specs=[WHOLE] * 3,
         out_specs=WHOLE,
         out_shape=pltpu.VMEM((2, count, width), BF16),
+        scratch_shapes=[
+            pltpu.VMEM((DEPTH, count), F32),
+            pltpu.VMEM((count, DEPTH), BF16),
+            pltpu.VMEM((count, 8), F32),
+        ],
         compiler_params=pltpu.CompilerParams(vmem_limit_bytes=8 * 2**20),
         cost_estimate=pl.CostEstimate(
             flops=2 * count * width * DEPTH,
@@ -180,7 +199,7 @@
             transcendentals=count * width,
         ),
         name="build_features",
-    )(left, right)
+    )(marks, right, norm)
 
 
 def spread_half(parts, half, values, other):
@@ -200,11 +219,10 @@
         for place, part_ref in enumerate(refs[:-1]):
             for start in range(0, count, tile):
                 at = slice(start, start + tile)
-                high, low = split(values_ref[:, place * count + start : place * count + start + tile])
-                both = jnp.concatenate([high, low], 0)
-                first = jnp.dot(both, part_ref[0, at, cols], preferred_element_type=F32)
-                second = jnp.dot(high, part_ref[1, at, cols], preferred_element_type=F32)
-                out_ref[:, :width] += first[:rows] + first[rows:] + second
+                left_rows = split_rows(values_ref[:, place * count + start : place * count + start + tile])
+                first = jnp.dot(left_rows, part_ref[0, at, cols], preferred_element_type=F32)
+                second = jnp.dot(left_rows[: 2 * rows], part_ref[1, at, cols], preferred_element_type=F32)
+                out_ref[:, :width] += add_rows(first, second, rows)
 
     return pl.pallas_call(
         kernel,
@@ -227,20 +245,19 @@
         cols = pl.ds(pl.multiple_of(half_ref[0] * width, width), width)
         v = values_ref[...]
         out_ref[:, lands:] = from_ref[:, lands:] + jnp.sum(v * v, 1, keepdims=True)
-        high, low = split(v)
-        both = jnp.concatenate([high, low], 0)
+        left_rows = split_rows(v)
         across = (((1,), (1,)), ((), ()))
         for place, part_ref in enumerate(refs[:-1]):
             for start in range(0, count, tile):
                 at = slice(start, start + tile)
                 first = lax.dot_general(
-                    both, part_ref[0, at, cols], across, preferred_element_type=F32
+                    left_rows, part_ref[0, at, cols], across, preferred_element_type=F32
                 )
                 second = lax.dot_general(
-                    high, part_ref[1, at, cols], across, preferred_element_type=F32
+                    left_rows[: 2 * rows], part_ref[1, at, cols], across, preferred_element_type=F32
                 )
                 to = slice(place * count + start, place * count + start + tile)
-                out_ref[:, to] = from_ref[:, to] + first[:rows] + first[rows:] + second
+                out_ref[:, to] = from_ref[:, to] + add_rows(first, second, rows)
 
     return pl.pallas_call(
         kernel,
@@ -283,20 +300,29 @@
     )
 
 
-def total_by_halves(x, axis, beside):
+def total_by_halves(maker, axis, early, late):
     here = lax.axis_index(axis)
-    for bit in bits(axis):
+    upper = (here & 1) != 0
+    send = maker(~upper)
+    upper, send = lax.optimization_barrier((upper, send))
+    other = swap(send, axis, 1)
+    x = maker(upper) + other
+    halvings = bits(axis)[1:]
+    for bit in halvings:
         half = x.shape[1] // 2
         upper = (here & bit) != 0
         keep = jnp.where(upper, x[:, half:], x[:, :half])
         send = jnp.where(upper, x[:, :half], x[:, half:])
         other = swap(send, axis, bit)
-        if bit == 1:
-            keep, beside = lax.optimization_barrier((keep, beside))
+        if bit == halvings[-1]:
+            keep, early = lax.optimization_barrier((keep, early))
         x = keep + other
-    for bit in reversed(bits(axis)[1:]):
-        x = in_order((here & bit) != 0, x, swap(x, axis, bit))
-    return x, swap(x, axis, 1), beside
+    for bit in reversed(halvings):
+        other = swap(x, axis, bit)
+        if bit == halvings[0]:
+            x, late = lax.optimization_barrier((x, late))
+        x = in_order((here & bit) != 0, x, other)
+    return x, swap(x, axis, 1), early, late
 
 
 def per_device(state, next_value, brownian, land_index):
@@ -305,44 +331,48 @@
     half = rows // 2
     paths = rows * lax.axis_size("path")
     landmarks = lands * lax.axis_size("land")
-    top = 8.0 * LOG2E - 0.5 * math.log2(landmarks)
+    top, scale = 0.0, math.exp(8.0) / math.sqrt(landmarks)
 
     here = lax.axis_index("path")
     core = lax.axis_index("land") & 1
     mine, its = core[None], 1 - core[None]
-    picked = pick(state, (land_index - here * rows)[None, :])
-    path_right = prepare(state, top, True, False)
-    path_left = prepare(state, top, True, True)
+    path_right = prepare(state)
+    path_norm = top - rate_of(state) * jnp.sum(state * state, 0, keepdims=True)
+    path_norm = jnp.broadcast_to(path_norm, (8, rows))
     targets = jnp.concatenate([next_value[None, :], next_value[None, :] * brownian], 0)
 
-    marks_own, marks_other, (path_right, path_left, targets) = total_by_halves(
-        picked, "path", (path_right, path_left, targets)
+    marks_own, marks_other, (path_right, path_norm), targets = total_by_halves(
+        lambda upper: pick(
+            state, jnp.where(upper, land_index[lands // 2 :], land_index[: lands // 2])[None, :] - here * rows
+        ),
+        "path",
+        (path_right, path_norm),
+        targets,
     )
     upper = (here & 1) != 0
-    sums = [gather_block(path_left, block, targets, top) for block in (marks_own, marks_other)]
+    sums = [gather_block(path_right, path_norm, block, targets, top) for block in (marks_own, marks_other)]
     marks = in_order(upper, marks_own, marks_other)
     rhs_part = in_order(upper, *sums)
     marks, rhs_part = lax.optimization_barrier((marks, rhs_part))
-    mark_left = prepare(marks, top, False, True)
     chunk = max(lands // 4, 256)
     parts = [
-        build_features(mark_left[start : start + chunk], path_right, top)
+        build_features(marks[:, start : start + chunk], path_right, path_norm, top)
         for start in range(0, lands, chunk)
     ]
-    rhs = total(rhs_part, "path") / paths
+    rhs = total(rhs_part, "path") * (scale / paths)
 
     def spread(values, other):
         theirs = spread_half(parts, its, values, other)
         ours = spread_half(parts, mine, values, other)
         ours = total(ours + swap(theirs, "land", 1), "land", 2)
-        return ours[:, :half], ours[:, half:]
+        return ours[:, :half] * scale, ours[:, half:]
 
     first, tail = spread(rhs, rhs)
     norm = tail[:, :1]
     first_other = swap(first, "land", 1)
     back = gather_half(parts, mine, first, jnp.zeros((rhs.shape[0], lands + 128), F32))
     back = total(gather_half(parts, its, first_other, back), "path")
-    image = back[:, :lands] / paths + LAMBDA_REG * rhs
+    image = back[:, :lands] * (scale / paths) + LAMBDA_REG * rhs
     alpha = norm / (back[:, lands : lands + 1] / paths + LAMBDA_REG * norm)
     resid = rhs - alpha * image
     second, tail = spread(resid, rhs)

time: 140 us -> 151 us (1.079)
  Pallas kernels: 49 us -> 63.8 us
  waiting for transfers between devices: 53.8 us -> 46.3 us
  starting transfers between devices: 26.6 us -> 29.6 us
  other arithmetic: 4.55 us -> 6.61 us
  local copies, waits for them, and re-layouts: 5.44 us -> 3.67 us
    pallas_call x6, Pallas kernels: 21.9 us -> 35 us  [the longest x2 20.8 us: gather_block(): pl.pallas_call(kernel, in_specs=[WHOLE] * 4, out_specs=WHOLE, out_shape=j...]
    ppermute x21, waiting for transfers between devices: 53.8 us -> 46.3 us  [swap(): return lax.ppermute(x, axis, [(i, i ^ bit) for i in range(count)])]
    ppermute x21, starting transfers between devices: 26.6 us -> 29.6 us  [swap(): return lax.ppermute(x, axis, [(i, i ^ bit) for i in range(count)])]
    unnamed x8 -> x10, local copies, waits for them, and re-layouts: 5.27 us -> 3.54 us
    select_n x5, other arithmetic: 0.8 us -> 2.52 us  [in_order(): jnp.where(upper, jnp.concatenate([other, own], 1), jnp.concatenate([own,...]
    pallas_call x1 -> x2, Pallas kernels: 5.41 us -> 6.81 us  [pick(): pl.pallas_call(kernel, in_specs=[WHOLE] * 2, out_specs=WHOLE, out_shape=j...]
  transfers between devices with their start and end apart: 21 -> 21, of which waited for: 14 -> 16; matrix products, arithmetic and copies ran while one was open for 1% -> 1% of each run, Pallas kernels for 19% -> 24%
where the time goes in v3:
time: 151 us; the launch traced here: 150 us
  Pallas kernels  63.8 us (42%)
  waiting for transfers between devices  46.3 us (31%)
  starting transfers between devices  29.6 us (20%)
  other arithmetic  6.61 us (4%)
  local copies, waits for them, and re-layouts  3.67 us (2%)
    ppermute x21, waiting for transfers between devices, swap(): return lax.ppermute(x, axis, [(i, i ^ bit) for i in range(count)])  46.3 us
    ppermute x21, starting transfers between devices, swap(): return lax.ppermute(x, axis, [(i, i ^ bit) for i in range(count)])  29.6 us
    pallas_call x2, Pallas kernels, gather_block(): pl.pallas_call(kernel, in_specs=[WHOLE] * 4, out_specs=WHOLE, out_shape=j...  20.8 us
    pallas_call x4, Pallas kernels, build_features(): pl.pallas_call(kernel, in_specs=[WHOLE] * 3, out_specs=WHOLE, out_shape=p...  14.2 us
    pallas_call x4, Pallas kernels, spread_half(): pl.pallas_call(kernel, in_specs=[pl.BlockSpec(memory_space=pltpu.SMEM)] +...  11.1 us
    pallas_call x2, Pallas kernels, gather_half(): pl.pallas_call(kernel, in_specs=[pl.BlockSpec(memory_space=pltpu.SMEM)] +...  9.77 us
    pallas_call x2, Pallas kernels, pick(): pl.pallas_call(kernel, in_specs=[WHOLE] * 2, out_specs=WHOLE, out_shape=j...  6.81 us
    unnamed x10, local copies, waits for them, and re-layouts  3.54 us
  transfers between devices with their start and end apart: 21, of which 16 were waited for; matrix products, arithmetic and copies ran while one was open for 1% of the time, Pallas kernels for 24%

profile of v3, /device:TPU:0, one launch (start us, length us, event | category | flops | bytes accessed | tf_op | source)
XLA Modules:
  0.0 150.3 jit_solution(14053438675078930908)
XLA Ops:
  1.9 3.4 %pick.2 = f32[50,1024]{1,0:T(8,128)S(1)} custom-call(f32[50,4096]{1,0:T(8,128)S(1)} %copy-done, s32[1,1024]{1,0:T(1,128)S(1)} %bitcast.4), custom_call_target="tpu_custom_call" | custom-call | tf_op jit(solution)/shard_map/pick/pallas_call | solution.py:150
  5.3 3.0 %collective-permute-start = (f32[50,1024]{1,0:T(8,128)S(1)}, f32[50,1024]{1,0:T(8,128)S(1)}, u32[]{:S(2)}, u32[]{:S(2)}) collective-permute-start(f32[50,1024]{1,0:T(8,128)S(1)} %pick.2), channel_id=1, source_target_pairs={{0,4},{4,0},{8,12},{12,8},{16,20},{20,16},{24,28},{28,24},{1,5},{5... | collective-permute-start | bytes 614408 | tf_op jit(solution)/shard_map/ppermute | solution.py:279
  10.2 3.4 %pick.3 = f32[50,1024]{1,0:T(8,128)S(1)} custom-call(f32[50,4096]{1,0:T(8,128)S(1)} %copy-done.1, s32[1,1024]{1,0:T(1,128)S(1)} %bitcast.5), custom_call_target="tpu_custom_call" | custom-call | tf_op jit(solution)/shard_map/pick/pallas_call | solution.py:150
  18.9 2.8 %collective-permute-start.2 = (f32[50,256]{1,0:T(8,128)S(1)}, f32[50,256]{1,0:T(8,128)S(1)}, u32[]{:S(2)}, u32[]{:S(2)}) collective-permute-start(f32[50,256]{1,0:T(8,128)S(1)} %get-tuple-element.27), channel_id=1, source_target_pairs={{0,16},{4,20},{8,24},{12,28},{16,0},{20,4},{24,8},{28,12},{1,17},{... | collective-permute-start | bytes 153608 | tf_op jit(solution)/shard_map/ppermute | solution.py:279
  24.1 2.9 %collective-permute-start.3 = (f32[50,256]{1,0:T(8,128)S(1)}, f32[50,256]{1,0:T(8,128)S(1)}, u32[]{:S(2)}, u32[]{:S(2)}) collective-permute-start(f32[50,256]{1,0:T(8,128)S(1)} %add.80), channel_id=1, source_target_pairs={{0,16},{4,20},{8,24},{12,28},{16,0},{20,4},{24,8},{28,12},{1,17},{... | collective-permute-start | bytes 153608 | tf_op jit(solution)/shard_map/ppermute | solution.py:279
  27.0 2.2 %collective-permute-done.3 = f32[50,256]{1,0:T(8,128)S(1)} collective-permute-done((f32[50,256]{1,0:T(8,128)S(1)}, f32[50,256]{1,0:T(8,128)S(1)}, u32[]{:S(2)}, u32[]{:S(2)}) %collective-permute-start.3) | collective-permute-done | bytes 51232 | tf_op jit(solution)/shard_map/ppermute | solution.py:279
  29.9 3.0 %collective-permute-start.4 = (f32[50,512]{1,0:T(8,128)}, f32[50,512]{1,0:T(8,128)}, u32[]{:S(2)}, u32[]{:S(2)}) collective-permute-start(f32[50,512]{1,0:T(8,128)} %maximum_select_fusion.4), channel_id=1, source_target_pairs={{0,8},{4,12},{8,0},{12,4},{16,24},{20,28},{24,16},{28,20},{1,9},{5... | collective-permute-start | bytes 307208 | tf_op jit(solution)/shard_map/ppermute | solution.py:279
  32.9 3.0 %collective-permute-done.4 = f32[50,512]{1,0:T(8,128)} collective-permute-done((f32[50,512]{1,0:T(8,128)}, f32[50,512]{1,0:T(8,128)}, u32[]{:S(2)}, u32[]{:S(2)}) %collective-permute-start.4) | collective-permute-done | bytes 102432 | tf_op jit(solution)/shard_map/ppermute | solution.py:279
  37.1 1.9 %collective-permute-start.5 = (f32[50,1024]{1,0:T(8,128)S(1)}, f32[50,1024]{1,0:T(8,128)S(1)}, u32[]{:S(2)}, u32[]{:S(2)}) collective-permute-start(f32[50,1024]{1,0:T(8,128)S(1)} %maximum_select_fusion.2.marks_ref), channel_id=1, source_target_pairs={{0,4},{4,0},{8,12},{12,8},{16,20},{20,16},{24,28},{28,24},{1,5},{5... | collective-permute-start | bytes 614408 | tf_op jit(solution)/shard_map/ppermute | solution.py:279
  39.0 10.4 %gather_block.3 = f32[16,1024]{1,0:T(8,128)S(1)} custom-call(bf16[384,4096]{1,0:T(8,128)(2,1)S(1)} %prepare.1.paths_ref.right_ref, f32[8,4096]{1,0:T(8,128)S(1)} %broadcast_in_dim.11.norm_ref, f32[50,1024]{1,0:T(8,128)S(1)} %maximum_select_fusion.2.marks_ref, f32[16,4096]{1,0:T(8,128)S(1)} %pad_maximum_fusion.values_ref), custom_call_target="tpu_custom_call" | custom-call | flops 6442450944 | bytes 6291456 | tf_op jit(solution)/shard_map/gather_block/pallas_call | solution.py:108
  49.4 10.4 %gather_block.2 = f32[16,1024]{1,0:T(8,128)S(1)} custom-call(bf16[384,4096]{1,0:T(8,128)(2,1)S(1)} %prepare.1.paths_ref.right_ref, f32[8,4096]{1,0:T(8,128)S(1)} %broadcast_in_dim.11.norm_ref, f32[50,1024]{1,0:T(8,128)S(1)} %collective-permute-done.5.marks_ref, f32[16,4096]{1,0:T(8,128)S(1)} %pad_maximum_fusion.values_ref), custom_call_target="tpu_custom_call" | custom-call | flops 6442450944 | bytes 6291456 | tf_op jit(solution)/shard_map/gather_block/pallas_call | solution.py:108
  59.9 3.5 %build_features.6.refs_2_ = bf16[2,512,4096]{2,1,0:T(8,128)(2,1)S(1)} custom-call(f32[50,512]{1,0:T(8,128)S(1)} %get-tuple-element.24.marks_ref, bf16[384,4096]{1,0:T(8,128)(2,1)S(1)} %prepare.1.paths_ref.right_ref, f32[8,4096]{1,0:T(8,128)S(1)} %broadcast_in_dim.11.norm_ref), custom_call_target="tpu_custom_call" | custom-call | flops 1610612736 | bytes 16777216 | tf_op jit(solution)/shard_map/build_features/pallas_call | solution.py:185
  63.6 3.5 %build_features.7.refs_3_ = bf16[2,512,4096]{2,1,0:T(8,128)(2,1)S(1)} custom-call(f32[50,512]{1,0:T(8,128)S(1)} %get-tuple-element.23.marks_ref, bf16[384,4096]{1,0:T(8,128)(2,1)S(1)} %prepare.1.paths_ref.right_ref, f32[8,4096]{1,0:T(8,128)S(1)} %broadcast_in_dim.11.norm_ref), custom_call_target="tpu_custom_call" | custom-call | flops 1610612736 | bytes 16777216 | tf_op jit(solution)/shard_map/build_features/pallas_call | solution.py:185
  68.4 2.1 %collective-permute-start.7 = (f32[16,2048]{1,0:T(8,128)S(1)}, f32[16,2048]{1,0:T(8,128)S(1)}, u32[]{:S(2)}, u32[]{:S(2)}) collective-permute-start(f32[16,2048]{1,0:T(8,128)S(1)} %add.81), channel_id=1, source_target_pairs={{0,8},{4,12},{8,0},{12,4},{16,24},{20,28},{24,16},{28,20},{1,9},{5... | collective-permute-start | bytes 393224 | tf_op jit(solution)/shard_map/ppermute | solution.py:279
  70.5 3.5 %build_features.5.refs_1_ = bf16[2,512,4096]{2,1,0:T(8,128)(2,1)S(1)} custom-call(f32[50,512]{1,0:T(8,128)S(1)} %get-tuple-element.25.marks_ref, bf16[384,4096]{1,0:T(8,128)(2,1)S(1)} %prepare.1.paths_ref.right_ref, f32[8,4096]{1,0:T(8,128)S(1)} %broadcast_in_dim.11.norm_ref), custom_call_target="tpu_custom_call" | custom-call | flops 1610612736 | bytes 16777216 | tf_op jit(solution)/shard_map/build_features/pallas_call | solution.py:185
  74.5 2.3 %collective-permute-start.8 = (f32[16,2048]{1,0:T(8,128)S(1)}, f32[16,2048]{1,0:T(8,128)S(1)}, u32[]{:S(2)}, u32[]{:S(2)}) collective-permute-start(f32[16,2048]{1,0:T(8,128)S(1)} %add.82), channel_id=1, source_target_pairs={{0,16},{4,20},{8,24},{12,28},{16,0},{20,4},{24,8},{28,12},{1,17},{... | collective-permute-start | bytes 393224 | tf_op jit(solution)/shard_map/ppermute | solution.py:279
  76.8 3.7 %build_features.4.refs_0_ = bf16[2,512,4096]{2,1,0:T(8,128)(2,1)S(1)} custom-call(f32[50,512]{1,0:T(8,128)S(1)} %get-tuple-element.26.marks_ref, bf16[384,4096]{1,0:T(8,128)(2,1)S(1)} %prepare.1.paths_ref.right_ref, f32[8,4096]{1,0:T(8,128)S(1)} %broadcast_in_dim.11.norm_ref), custom_call_target="tpu_custom_call" | custom-call | flops 1610612736 | bytes 16777216 | tf_op jit(solution)/shard_map/build_features/pallas_call | solution.py:185
  81.8 2.7 %spread_half.5 = f32[16,2176]{1,0:T(8,128)S(1)} custom-call(s32[1]{0:T(128)S(6)} %sub.38.half_ref, f32[16,2048]{1,0:T(8,128)S(1)} %broadcast_multiply_fusion.1.values_ref.other_ref, f32[16,2048]{1,0:T(8,128)S(1)} %broadcast_multiply_fusion.1.values_ref.other_ref, bf16[2,512,4096]{2,1,0:T(8,128)(2,1)S(1)} %build_features.4.refs_0_, ...), custom_call_target="tpu_custom_call" | custom-call | tf_op jit(solution)/shard_map/spread_half/pallas_call | solution.py:227
  84.6 2.7 %spread_half.4 = f32[16,2176]{1,0:T(8,128)S(1)} custom-call(s32[1]{0:T(128)} %bitcast.half_ref, f32[16,2048]{1,0:T(8,128)S(1)} %broadcast_multiply_fusion.1.values_ref.other_ref, f32[16,2048]{1,0:T(8,128)S(1)} %broadcast_multiply_fusion.1.values_ref.other_ref, bf16[2,512,4096]{2,1,0:T(8,128)(2,1)S(1)} %build_features.4.refs_0_, ...), custom_call_target="tpu_custom_call" | custom-call | tf_op jit(solution)/shard_map/spread_half/pallas_call | solution.py:227
  88.9 4.6 %collective-permute-done.10 = f32[16,2176]{1,0:T(8,128)S(1)} collective-permute-done((f32[16,2176]{1,0:T(8,128)S(1)}, f32[16,2176]{1,0:T(8,128)S(1)}, u32[]{:S(2)}, u32[]{:S(2)}) %collective-permute-start.10) | collective-permute-done | bytes 139296 | tf_op jit(solution)/shard_map/ppermute | solution.py:279
  93.6 4.9 %gather_half.2.from_ref = f32[16,2176]{1,0:T(8,128)S(1)} custom-call(s32[1]{0:T(128)} %bitcast.half_ref, f32[16,2048]{1,0:T(8,128)S(1)} %slice_multiply_fusion.2.values_ref, f32[16,2176]{1,0:T(8,128)S(1)} %broadcast_in_dim.13.from_ref, bf16[2,512,4096]{2,1,0:T(8,128)(2,1)S(1)} %build_features.4.refs_0_, bf16[2,512,4096]{2,1,0:T(8,128)(2,1)S(1)} %build_features.5.refs_1_, ...), custom_call_target="tpu_custom_call" | custom-call | flops 3221225472 | bytes 16777216 | tf_op jit(solution)/shard_map/gather_half/pallas_call | solution.py:262
  98.5 4.9 %gather_half.3 = f32[16,2176]{1,0:T(8,128)S(1)} custom-call(s32[1]{0:T(128)S(6)} %sub.38.half_ref, f32[16,2048]{1,0:T(8,128)S(1)} %collective-permute-done.11.values_ref, f32[16,2176]{1,0:T(8,128)S(1)} %gather_half.2.from_ref, bf16[2,512,4096]{2,1,0:T(8,128)(2,1)S(1)} %build_features.4.refs_0_, bf16[2,512,4096]{2,1,0:T(8,128)(2,1)S(1)} %build_features.5.refs_1_, ...), custom_call_target="tpu_custom_call" | custom-call | flops 3221225472 | bytes 16777216 | tf_op jit(solution)/shard_map/gather_half/pallas_call | solution.py:262
  104.4 5.1 %collective-permute-done.12 = f32[16,2176]{1,0:T(8,128)S(1)} collective-permute-done((f32[16,2176]{1,0:T(8,128)S(1)}, f32[16,2176]{1,0:T(8,128)S(1)}, u32[]{:S(2)}, u32[]{:S(2)}) %collective-permute-start.12) | collective-permute-done | bytes 139296 | tf_op jit(solution)/shard_map/ppermute | solution.py:279
  109.9 5.0 %collective-permute-done.13 = f32[16,2176]{1,0:T(8,128)S(1)} collective-permute-done((f32[16,2176]{1,0:T(8,128)S(1)}, f32[16,2176]{1,0:T(8,128)S(1)}, u32[]{:S(2)}, u32[]{:S(2)}) %collective-permute-start.13) | collective-permute-done | bytes 139296 | tf_op jit(solution)/shard_map/ppermute | solution.py:279
  114.9 2.0 %collective-permute-start.14 = (f32[16,2176]{1,0:T(8,128)S(1)}, f32[16,2176]{1,0:T(8,128)S(1)}, u32[]{:S(2)}, u32[]{:S(2)}) collective-permute-start(f32[16,2176]{1,0:T(8,128)S(1)} %add.87), channel_id=1, source_target_pairs={{0,16},{4,20},{8,24},{12,28},{16,0},{20,4},{24,8},{28,12},{1,17},{... | collective-permute-start | bytes 417800 | tf_op jit(solution)/shard_map/ppermute | solution.py:279
  116.9 6.3 %collective-permute-done.14 = f32[16,2176]{1,0:T(8,128)S(1)} collective-permute-done((f32[16,2176]{1,0:T(8,128)S(1)}, f32[16,2176]{1,0:T(8,128)S(1)}, u32[]{:S(2)}, u32[]{:S(2)}) %collective-permute-start.14) | collective-permute-done | bytes 139296 | tf_op jit(solution)/shard_map/ppermute | solution.py:279
  123.5 2.9 %spread_half.7 = f32[16,2176]{1,0:T(8,128)S(1)} custom-call(s32[1]{0:T(128)S(6)} %sub.38.half_ref, f32[16,2048]{1,0:T(8,128)S(1)} %fusion.2.values_ref, f32[16,2048]{1,0:T(8,128)S(1)} %broadcast_multiply_fusion.1.values_ref.other_ref, bf16[2,512,4096]{2,1,0:T(8,128)(2,1)S(1)} %build_features.4.refs_0_, bf16[2,512,4096]{2,1,0:T(8,128)(2,1)S(1)} %build_features.5.refs_1_, ...), custom_call_target="tpu_custom_call" | custom-call | tf_op jit(solution)/shard_map/spread_half/pallas_call | solution.py:227
  126.4 2.7 %spread_half.6 = f32[16,2176]{1,0:T(8,128)S(1)} custom-call(s32[1]{0:T(128)} %bitcast.half_ref, f32[16,2048]{1,0:T(8,128)S(1)} %fusion.2.values_ref, f32[16,2048]{1,0:T(8,128)S(1)} %broadcast_multiply_fusion.1.values_ref.other_ref, bf16[2,512,4096]{2,1,0:T(8,128)(2,1)S(1)} %build_features.4.refs_0_, bf16[2,512,4096]{2,1,0:T(8,128)(2,1)S(1)} %build_features.5.refs_1_, ...), custom_call_target="tpu_custom_call" | custom-call | tf_op jit(solution)/shard_map/spread_half/pallas_call | solution.py:227
  130.8 4.6 %collective-permute-done.16 = f32[16,2176]{1,0:T(8,128)S(1)} collective-permute-done((f32[16,2176]{1,0:T(8,128)S(1)}, f32[16,2176]{1,0:T(8,128)S(1)}, u32[]{:S(2)}, u32[]{:S(2)}) %collective-permute-start.16) | collective-permute-done | bytes 139296 | tf_op jit(solution)/shard_map/ppermute | solution.py:279
  138.1 2.7 %collective-permute-done.18 = f32[16,128]{1,0:T(8,128)S(1)} collective-permute-done((f32[16,128]{1,0:T(8,128)S(1)}, f32[16,128]{1,0:T(8,128)S(1)}, u32[]{:S(2)}, u32[]{:S(2)}) %collective-permute-start.18) | collective-permute-done | bytes 8224 | tf_op jit(solution)/shard_map/ppermute | solution.py:279
  141.3 3.3 %collective-permute-done.19 = f32[16,128]{1,0:T(8,128)S(1)} collective-permute-done((f32[16,128]{1,0:T(8,128)S(1)}, f32[16,128]{1,0:T(8,128)S(1)}, u32[]{:S(2)}, u32[]{:S(2)}) %collective-permute-start.19) | collective-permute-done | bytes 8224 | tf_op jit(solution)/shard_map/ppermute | solution.py:279
  146.3 2.9 %collective-permute-done.20 = f32[16,128]{1,0:T(8,128)S(1)} collective-permute-done((f32[16,128]{1,0:T(8,128)S(1)}, f32[16,128]{1,0:T(8,128)S(1)}, u32[]{:S(2)}, u32[]{:S(2)}) %collective-permute-start.20) | collective-permute-done | bytes 8224 | tf_op jit(solution)/shard_map/ppermute | solution.py:279
  (77 shorter events, 27.4 us)
Async XLA Ops:
  0.0 27.0 %copy-start.4 = (f32[4096]{0:T(1024)S(1)}, f32[4096]{0:T(1024)}, u32[]{:S(2)}) copy-start(f32[4096]{0:T(1024)} %param.5) | copy-start | bytes 49156
  0.7 1.2 copy-start
  1.9 25.1 %copy-start.3 = (f32[15,4096]{1,0:T(8,128)S(1)}, f32[15,4096]{1,0:T(8,128)}, u32[]{:S(2)}) copy-start(f32[15,4096]{1,0:T(8,128)} %param.6) | copy-start | bytes 737284
  5.3 8.7 %collective-permute-start = (f32[50,1024]{1,0:T(8,128)S(1)}, f32[50,1024]{1,0:T(8,128)S(1)}, u32[]{:S(2)}, u32[]{:S(2)}) collective-permute-start(f32[50,1024]{1,0:T(8,128)S(1)} %pick.2), channel_id=1, source_target_pairs={{0,4},{4,0},{8,12},{12,8},{16,20},{20,16},{24,28},{28,24},{1,5},{5... | collective-permute-start | bytes 614408 | tf_op jit(solution)/shard_map/ppermute | solution.py:279
  9.1 1.2 copy-start.1
  14.0 4.9 %collective-permute-start.1 = (f32[50,512]{1,0:T(8,128)S(1)}, f32[50,512]{1,0:T(8,128)S(1)}, u32[]{:S(2)}, u32[]{:S(2)}) collective-permute-start(f32[50,512]{1,0:T(8,128)S(1)} %slice_select_fusion), channel_id=1, source_target_pairs={{0,8},{4,12},{8,0},{12,4},{16,24},{20,28},{24,16},{28,20},{1,9},{5... | collective-permute-start | bytes 307208 | tf_op jit(solution)/shard_map/ppermute | solution.py:279
  18.9 5.1 %collective-permute-start.2 = (f32[50,256]{1,0:T(8,128)S(1)}, f32[50,256]{1,0:T(8,128)S(1)}, u32[]{:S(2)}, u32[]{:S(2)}) collective-permute-start(f32[50,256]{1,0:T(8,128)S(1)} %get-tuple-element.27), channel_id=1, source_target_pairs={{0,16},{4,20},{8,24},{12,28},{16,0},{20,4},{24,8},{28,12},{1,17},{... | collective-permute-start | bytes 153608 | tf_op jit(solution)/shard_map/ppermute | solution.py:279
  21.8 1.2 copy-start.2
  24.1 5.1 %collective-permute-start.3 = (f32[50,256]{1,0:T(8,128)S(1)}, f32[50,256]{1,0:T(8,128)S(1)}, u32[]{:S(2)}, u32[]{:S(2)}) collective-permute-start(f32[50,256]{1,0:T(8,128)S(1)} %add.80), channel_id=1, source_target_pairs={{0,16},{4,20},{8,24},{12,28},{16,0},{20,4},{24,8},{28,12},{1,17},{... | collective-permute-start | bytes 153608 | tf_op jit(solution)/shard_map/ppermute | solution.py:279
  29.9 6.0 %collective-permute-start.4 = (f32[50,512]{1,0:T(8,128)}, f32[50,512]{1,0:T(8,128)}, u32[]{:S(2)}, u32[]{:S(2)}) collective-permute-start(f32[50,512]{1,0:T(8,128)} %maximum_select_fusion.4), channel_id=1, source_target_pairs={{0,8},{4,12},{8,0},{12,4},{16,24},{20,28},{24,16},{28,20},{1,9},{5... | collective-permute-start | bytes 307208 | tf_op jit(solution)/shard_map/ppermute | solution.py:279
  37.1 12.3 %collective-permute-start.5 = (f32[50,1024]{1,0:T(8,128)S(1)}, f32[50,1024]{1,0:T(8,128)S(1)}, u32[]{:S(2)}, u32[]{:S(2)}) collective-permute-start(f32[50,1024]{1,0:T(8,128)S(1)} %maximum_select_fusion.2.marks_ref), channel_id=1, source_target_pairs={{0,4},{4,0},{8,12},{12,8},{16,20},{20,16},{24,28},{28,24},{1,5},{5... | collective-permute-start | bytes 614408 | tf_op jit(solution)/shard_map/ppermute | solution.py:279
  63.4 5.0 %collective-permute-start.6 = (f32[16,2048]{1,0:T(8,128)S(1)}, f32[16,2048]{1,0:T(8,128)S(1)}, u32[]{:S(2)}, u32[]{:S(2)}) collective-permute-start(f32[16,2048]{1,0:T(8,128)S(1)} %maximum_select_fusion.3), channel_id=1, source_target_pairs={{0,4},{4,0},{8,12},{12,8},{16,20},{20,16},{24,28},{28,24},{1,5},{5... | collective-permute-start | bytes 393224 | tf_op jit(solution)/shard_map/ppermute | solution.py:279
  68.4 6.0 %collective-permute-start.7 = (f32[16,2048]{1,0:T(8,128)S(1)}, f32[16,2048]{1,0:T(8,128)S(1)}, u32[]{:S(2)}, u32[]{:S(2)}) collective-permute-start(f32[16,2048]{1,0:T(8,128)S(1)} %add.81), channel_id=1, source_target_pairs={{0,8},{4,12},{8,0},{12,4},{16,24},{20,28},{24,16},{28,20},{1,9},{5... | collective-permute-start | bytes 393224 | tf_op jit(solution)/shard_map/ppermute | solution.py:279
  74.5 7.3 %collective-permute-start.8 = (f32[16,2048]{1,0:T(8,128)S(1)}, f32[16,2048]{1,0:T(8,128)S(1)}, u32[]{:S(2)}, u32[]{:S(2)}) collective-permute-start(f32[16,2048]{1,0:T(8,128)S(1)} %add.82), channel_id=1, source_target_pairs={{0,16},{4,20},{8,24},{12,28},{16,0},{20,4},{24,8},{28,12},{1,17},{... | collective-permute-start | bytes 393224 | tf_op jit(solution)/shard_map/ppermute | solution.py:279
  84.6 2.7 %collective-permute-start.9 = (f32[16,2176]{1,0:T(8,128)S(1)}, f32[16,2176]{1,0:T(8,128)S(1)}, u32[]{:S(2)}, u32[]{:S(2)}) collective-permute-start(f32[16,2176]{1,0:T(8,128)S(1)} %spread_half.5), channel_id=1, source_target_pairs={{0,1},{1,0},{2,3},{3,2},{4,5},{5,4},{6,7},{7,6},{8,9},{9,8},{10,11... | collective-permute-start | bytes 417800 | tf_op jit(solution)/shard_map/ppermute | solution.py:279
  87.3 6.2 %collective-permute-start.10 = (f32[16,2176]{1,0:T(8,128)S(1)}, f32[16,2176]{1,0:T(8,128)S(1)}, u32[]{:S(2)}, u32[]{:S(2)}) collective-permute-start(f32[16,2176]{1,0:T(8,128)S(1)} %add.84), channel_id=1, source_target_pairs={{0,2},{1,3},{2,0},{3,1},{4,6},{5,7},{6,4},{7,5},{8,10},{9,11},{10,... | collective-permute-start | bytes 417800 | tf_op jit(solution)/shard_map/ppermute | solution.py:279
  93.5 5.0 %collective-permute-start.11 = (f32[16,2048]{1,0:T(8,128)S(1)}, f32[16,2048]{1,0:T(8,128)S(1)}, u32[]{:S(2)}, u32[]{:S(2)}) collective-permute-start(f32[16,2048]{1,0:T(8,128)S(1)} %slice_multiply_fusion.2.values_ref), channel_id=1, source_target_pairs={{0,1},{1,0},{2,3},{3,2},{4,5},{5,4},{6,7},{7,6},{8,9},{9,8},{10,11... | collective-permute-start | bytes 393224 | tf_op jit(solution)/shard_map/ppermute | solution.py:279
  103.4 6.1 %collective-permute-start.12 = (f32[16,2176]{1,0:T(8,128)S(1)}, f32[16,2176]{1,0:T(8,128)S(1)}, u32[]{:S(2)}, u32[]{:S(2)}) collective-permute-start(f32[16,2176]{1,0:T(8,128)S(1)} %gather_half.3), channel_id=1, source_target_pairs={{0,4},{4,0},{8,12},{12,8},{16,20},{20,16},{24,28},{28,24},{1,5},{5... | collective-permute-start | bytes 417800 | tf_op jit(solution)/shard_map/ppermute | solution.py:279
  109.5 5.4 %collective-permute-start.13 = (f32[16,2176]{1,0:T(8,128)S(1)}, f32[16,2176]{1,0:T(8,128)S(1)}, u32[]{:S(2)}, u32[]{:S(2)}) collective-permute-start(f32[16,2176]{1,0:T(8,128)S(1)} %add.86), channel_id=1, source_target_pairs={{0,8},{4,12},{8,0},{12,4},{16,24},{20,28},{24,16},{28,20},{1,9},{5... | collective-permute-start | bytes 417800 | tf_op jit(solution)/shard_map/ppermute | solution.py:279
  114.9 8.4 %collective-permute-start.14 = (f32[16,2176]{1,0:T(8,128)S(1)}, f32[16,2176]{1,0:T(8,128)S(1)}, u32[]{:S(2)}, u32[]{:S(2)}) collective-permute-start(f32[16,2176]{1,0:T(8,128)S(1)} %add.87), channel_id=1, source_target_pairs={{0,16},{4,20},{8,24},{12,28},{16,0},{20,4},{24,8},{28,12},{1,17},{... | collective-permute-start | bytes 417800 | tf_op jit(solution)/shard_map/ppermute | solution.py:279
  126.4 2.8 %collective-permute-start.15 = (f32[16,2176]{1,0:T(8,128)S(1)}, f32[16,2176]{1,0:T(8,128)S(1)}, u32[]{:S(2)}, u32[]{:S(2)}) collective-permute-start(f32[16,2176]{1,0:T(8,128)S(1)} %spread_half.7), channel_id=1, source_target_pairs={{0,1},{1,0},{2,3},{3,2},{4,5},{5,4},{6,7},{7,6},{8,9},{9,8},{10,11... | collective-permute-start | bytes 417800 | tf_op jit(solution)/shard_map/ppermute | solution.py:279
  129.2 6.1 %collective-permute-start.16 = (f32[16,2176]{1,0:T(8,128)S(1)}, f32[16,2176]{1,0:T(8,128)S(1)}, u32[]{:S(2)}, u32[]{:S(2)}) collective-permute-start(f32[16,2176]{1,0:T(8,128)S(1)} %add.91), channel_id=1, source_target_pairs={{0,2},{1,3},{2,0},{3,1},{4,6},{5,7},{6,4},{7,5},{8,10},{9,11},{10,... | collective-permute-start | bytes 417800 | tf_op jit(solution)/shard_map/ppermute | solution.py:279
  135.5 1.4 collective-permute-start.17
  137.2 3.7 %collective-permute-start.18 = (f32[16,128]{1,0:T(8,128)S(1)}, f32[16,128]{1,0:T(8,128)S(1)}, u32[]{:S(2)}, u32[]{:S(2)}) collective-permute-start(f32[16,128]{1,0:T(8,128)S(1)} %broadcast_in_dim.14), channel_id=1, source_target_pairs={{0,4},{4,0},{8,12},{12,8},{16,20},{20,16},{24,28},{28,24},{1,5},{5... | collective-permute-start | bytes 24584 | tf_op jit(solution)/shard_map/ppermute | solution.py:279
  140.9 3.7 %collective-permute-start.19 = (f32[16,128]{1,0:T(8,128)S(1)}, f32[16,128]{1,0:T(8,128)S(1)}, u32[]{:S(2)}, u32[]{:S(2)}) collective-permute-start(f32[16,128]{1,0:T(8,128)S(1)} %broadcast_add_fusion), channel_id=1, source_target_pairs={{0,8},{4,12},{8,0},{12,4},{16,24},{20,28},{24,16},{28,20},{1,9},{5... | collective-permute-start | bytes 24584 | tf_op jit(solution)/shard_map/ppermute | solution.py:279
  144.7 4.6 %collective-permute-start.20 = (f32[16,128]{1,0:T(8,128)S(1)}, f32[16,128]{1,0:T(8,128)S(1)}, u32[]{:S(2)}, u32[]{:S(2)}) collective-permute-start(f32[16,128]{1,0:T(8,128)S(1)} %fusion.15), channel_id=1, source_target_pairs={{0,16},{4,20},{8,24},{12,28},{16,0},{20,4},{24,8},{28,12},{1,17},{... | collective-permute-start | bytes 24584 | tf_op jit(solution)/shard_map/ppermute | solution.py:279

commit v4 on v3

--- a/solution.py
+++ b/solution.py
@@ -38,28 +38,31 @@
     return first[:rows] + (first[rows : 2 * rows] + small)
 
 
-def rate_of(x):
-    return 4.0 * LOG2E / x.shape[0]
-
-
-def augment(ref, x, of_path):
-    dims = x.shape[0]
+def augment(ref, x, top, of_path):
+    dims, count = x.shape
+    rate = 4.0 * LOG2E / dims
+    norm = -rate * jnp.sum(x * x, 0, keepdims=True)
+    ones = jnp.ones((1, count), F32)
     if of_path:
-        high, middle, low = pieces(x * (2.0 * rate_of(x)), 3)
+        high, middle, low = pieces(x * (2.0 * rate), 3)
         bands = (high, high, middle, high, middle, low)
+        extra = pieces(norm + top, 3) + [ones] * 3
     else:
         high, middle, low = pieces(x, 3)
         bands = (high, middle, high, low, middle, high)
+        extra = [ones] * 3 + pieces(norm, 3)
     ref[...] = jnp.zeros_like(ref)
     for place, band in enumerate(bands):
         ref[place * BAND : place * BAND + dims, :] = band
-
-
-def prepare(x):
+    for place, row in enumerate(extra):
+        ref[dims + place : dims + place + 1, :] = row
+
+
+def prepare(x, top):
     count = x.shape[1]
 
     def kernel(x_ref, out_ref, full):
-        augment(full, x_ref[...], True)
+        augment(full, x_ref[...], top, True)
         out_ref[...] = full[...].astype(BF16)
 
     return pl.pallas_call(
@@ -76,16 +79,14 @@
     )(x)
 
 
-def gather_block(paths, norm, marks, values, top):
+def gather_block(paths, marks, values, top):
     depth, width = paths.shape[1], marks.shape[1]
     rows = values.shape[0]
     tile = min(512, depth)
     span = min(1024, width)
 
-    def kernel(paths_ref, norm_ref, marks_ref, values_ref, out_ref, full, right):
-        m = marks_ref[...]
-        augment(full, m, False)
-        mark_norm = -rate_of(m) * jnp.sum(m * m, 0, keepdims=True)
+    def kernel(paths_ref, marks_ref, values_ref, out_ref, full, right):
+        augment(full, marks_ref[...], top, False)
         right[...] = full[...].astype(BF16)
         out_ref[...] = jnp.zeros_like(out_ref)
 
@@ -93,12 +94,10 @@
         def _(i):
             at = pl.ds(pl.multiple_of(i * tile, tile), tile)
             left = paths_ref[:, at].astype(F32).T.astype(BF16)
-            norms = norm_ref[:, at].T[:, :1]
             left_rows = split_rows(values_ref[:, at])
             for start in range(0, width, span):
                 to = slice(start, start + span)
                 exponent = jnp.dot(left, right[:, to], preferred_element_type=F32)
-                exponent = exponent + (norms + mark_norm[:, to])
                 feat = jnp.exp2(jnp.minimum(exponent, top))
                 high, low = split(feat)
                 first = jnp.dot(left_rows, high, preferred_element_type=F32)
@@ -107,7 +106,7 @@
 
     return pl.pallas_call(
         kernel,
-        in_specs=[WHOLE] * 4,
+        in_specs=[WHOLE] * 3,
         out_specs=WHOLE,
         out_shape=jax.ShapeDtypeStruct((rows, width), F32),
         scratch_shapes=[pltpu.VMEM((DEPTH, width), F32), pltpu.VMEM((DEPTH, width), BF16)],
@@ -118,7 +117,7 @@
             transcendentals=depth * width,
         ),
         name="gather_block",
-    )(paths, norm, marks, values)
+    )(paths, marks, values)
 
 
 def pick(state, column):
@@ -161,22 +160,18 @@
     )(state, column)
 
 
-def build_features(marks, right, norm, top):
+def build_features(marks, right, top):
     count, width = marks.shape[1], right.shape[1]
     tile = min(256, count)
 
-    def kernel(marks_ref, right_ref, norm_ref, out_ref, full, left, norms):
-        m = marks_ref[...]
-        augment(full, m, False)
-        mark_norm = -rate_of(m) * jnp.sum(m * m, 0, keepdims=True)
-        norms[...] = jnp.broadcast_to(mark_norm, (8, count)).T
+    def kernel(marks_ref, right_ref, out_ref, full, left):
+        augment(full, marks_ref[...], top, False)
         left[...] = full[...].T.astype(BF16)
 
         @pl.loop(0, count // tile)
         def _(i):
             at = pl.ds(pl.multiple_of(i * tile, tile), tile)
             exponent = jnp.dot(left[at, :], right_ref[...], preferred_element_type=F32)
-            exponent = exponent + (norms[at, :1] + norm_ref[:1, :])
             feat = jnp.exp2(jnp.minimum(exponent, top))
             high, low = split(feat)
             out_ref[0, at, :] = high
@@ -184,14 +179,10 @@
 
     return pl.pallas_call(
         kernel,
-        in_specs=[WHOLE] * 3,
+        in_specs=[WHOLE] * 2,
         out_specs=WHOLE,
         out_shape=pltpu.VMEM((2, count, width), BF16),
-        scratch_shapes=[
-            pltpu.VMEM((DEPTH, count), F32),
-            pltpu.VMEM((count, DEPTH), BF16),
-            pltpu.VMEM((count, 8), F32),
-        ],
+        scratch_shapes=[pltpu.VMEM((DEPTH, count), F32), pltpu.VMEM((count, DEPTH), BF16)],
         compiler_params=pltpu.CompilerParams(vmem_limit_bytes=8 * 2**20),
         cost_estimate=pl.CostEstimate(
             flops=2 * count * width * DEPTH,
@@ -199,7 +190,7 @@
             transcendentals=count * width,
         ),
         name="build_features",
-    )(marks, right, norm)
+    )(marks, right)
 
 
 def spread_half(parts, half, values, other):
@@ -336,27 +327,25 @@
     here = lax.axis_index("path")
     core = lax.axis_index("land") & 1
     mine, its = core[None], 1 - core[None]
-    path_right = prepare(state)
-    path_norm = top - rate_of(state) * jnp.sum(state * state, 0, keepdims=True)
-    path_norm = jnp.broadcast_to(path_norm, (8, rows))
+    path_right = prepare(state, top)
     targets = jnp.concatenate([next_value[None, :], next_value[None, :] * brownian], 0)
 
-    marks_own, marks_other, (path_right, path_norm), targets = total_by_halves(
+    marks_own, marks_other, path_right, targets = total_by_halves(
         lambda upper: pick(
             state, jnp.where(upper, land_index[lands // 2 :], land_index[: lands // 2])[None, :] - here * rows
         ),
         "path",
-        (path_right, path_norm),
+        path_right,
         targets,
     )
     upper = (here & 1) != 0
-    sums = [gather_block(path_right, path_norm, block, targets, top) for block in (marks_own, marks_other)]
+    sums = [gather_block(path_right, block, targets, top) for block in (marks_own, marks_other)]
     marks = in_order(upper, marks_own, marks_other)
     rhs_part = in_order(upper, *sums)
     marks, rhs_part = lax.optimization_barrier((marks, rhs_part))
     chunk = max(lands // 4, 256)
     parts = [
-        build_features(marks[:, start : start + chunk], path_right, path_norm, top)
+        build_features(marks[:, start : start + chunk], path_right, top)
         for start in range(0, lands, chunk)
     ]
     rhs = total(rhs_part, "path") * (scale / paths)

time: 151 us -> 146 us (0.967)
  Pallas kernels: 63.8 us -> 58.9 us
  waiting for transfers between devices: 46.3 us -> 49.8 us
  starting transfers between devices: 29.6 us -> 27.6 us
    pallas_call x6, Pallas kernels: 35 us -> 29.9 us  [the longest x2 17.8 us: gather_block(): pl.pallas_call(kernel, in_specs=[WHOLE] * 3, out_specs=WHOLE, out_shape=j...]
    ppermute x21, waiting for transfers between devices: 46.3 us -> 49.8 us  [swap(): return lax.ppermute(x, axis, [(i, i ^ bit) for i in range(count)])]
    ppermute x21, starting transfers between devices: 29.6 us -> 27.6 us  [swap(): return lax.ppermute(x, axis, [(i, i ^ bit) for i in range(count)])]
  transfers between devices with their start and end apart: 21 -> 21, of which waited for: 16 -> 16; matrix products, arithmetic and copies ran while one was open for 1% -> 1% of each run, Pallas kernels for 24% -> 23%
where the time goes in v4:
time: 146 us
  Pallas kernels  58.9 us (40%)
  waiting for transfers between devices  49.8 us (34%)
  starting transfers between devices  27.6 us (19%)
  other arithmetic  5.32 us (4%)
  local copies, waits for them, and re-layouts  3.66 us (3%)
    ppermute x21, waiting for transfers between devices, swap(): return lax.ppermute(x, axis, [(i, i ^ bit) for i in range(count)])  49.8 us
    ppermute x21, starting transfers between devices, swap(): return lax.ppermute(x, axis, [(i, i ^ bit) for i in range(count)])  27.6 us
    pallas_call x2, Pallas kernels, gather_block(): pl.pallas_call(kernel, in_specs=[WHOLE] * 3, out_specs=WHOLE, out_shape=j...  17.8 us
    pallas_call x4, Pallas kernels, build_features(): pl.pallas_call(kernel, in_specs=[WHOLE] * 2, out_specs=WHOLE, out_shape=p...  12.1 us
    pallas_call x4, Pallas kernels, spread_half(): pl.pallas_call(kernel, in_specs=[pl.BlockSpec(memory_space=pltpu.SMEM)] +...  11.2 us
    pallas_call x2, Pallas kernels, gather_half(): pl.pallas_call(kernel, in_specs=[pl.BlockSpec(memory_space=pltpu.SMEM)] +...  9.77 us
    pallas_call x2, Pallas kernels, pick(): pl.pallas_call(kernel, in_specs=[WHOLE] * 2, out_specs=WHOLE, out_shape=j...  6.81 us
    unnamed x10, local copies, waits for them, and re-layouts  3.54 us
  transfers between devices with their start and end apart: 21, of which 16 were waited for; matrix products, arithmetic and copies ran while one was open for 1% of the time, Pallas kernels for 23%

profile of v4, /device:TPU:0, one launch (start us, length us, event | category | flops | bytes accessed | tf_op | source)
XLA Modules:
  0.0 145.5 jit_solution(4571110971424850321)
XLA Ops:
  1.9 3.4 %pick.2 = f32[50,1024]{1,0:T(8,128)S(1)} custom-call(f32[50,4096]{1,0:T(8,128)S(1)} %copy-done, s32[1,1024]{1,0:T(1,128)S(1)} %bitcast.4), custom_call_target="tpu_custom_call" | custom-call | tf_op jit(solution)/shard_map/pick/pallas_call | solution.py:149
  5.3 3.0 %collective-permute-start = (f32[50,1024]{1,0:T(8,128)S(1)}, f32[50,1024]{1,0:T(8,128)S(1)}, u32[]{:S(2)}, u32[]{:S(2)}) collective-permute-start(f32[50,1024]{1,0:T(8,128)S(1)} %pick.2), channel_id=1, source_target_pairs={{0,4},{4,0},{8,12},{12,8},{16,20},{20,16},{24,28},{28,24},{1,5},{5... | collective-permute-start | bytes 614408 | tf_op jit(solution)/shard_map/ppermute | solution.py:270
  10.2 3.4 %pick.3 = f32[50,1024]{1,0:T(8,128)S(1)} custom-call(f32[50,4096]{1,0:T(8,128)S(1)} %copy-done.1, s32[1,1024]{1,0:T(1,128)S(1)} %bitcast.5), custom_call_target="tpu_custom_call" | custom-call | tf_op jit(solution)/shard_map/pick/pallas_call | solution.py:149
  15.9 3.0 %collective-permute-done.1 = f32[50,512]{1,0:T(8,128)S(1)} collective-permute-done((f32[50,512]{1,0:T(8,128)S(1)}, f32[50,512]{1,0:T(8,128)S(1)}, u32[]{:S(2)}, u32[]{:S(2)}) %collective-permute-start.1) | collective-permute-done | bytes 102432 | tf_op jit(solution)/shard_map/ppermute | solution.py:270
  18.9 2.8 %collective-permute-start.2 = (f32[50,256]{1,0:T(8,128)S(1)}, f32[50,256]{1,0:T(8,128)S(1)}, u32[]{:S(2)}, u32[]{:S(2)}) collective-permute-start(f32[50,256]{1,0:T(8,128)S(1)} %get-tuple-element.25), channel_id=1, source_target_pairs={{0,16},{4,20},{8,24},{12,28},{16,0},{20,4},{24,8},{28,12},{1,17},{... | collective-permute-start | bytes 153608 | tf_op jit(solution)/shard_map/ppermute | solution.py:270
  24.3 2.7 %collective-permute-start.3 = (f32[50,256]{1,0:T(8,128)S(1)}, f32[50,256]{1,0:T(8,128)S(1)}, u32[]{:S(2)}, u32[]{:S(2)}) collective-permute-start(f32[50,256]{1,0:T(8,128)S(1)} %add.80), channel_id=1, source_target_pairs={{0,16},{4,20},{8,24},{12,28},{16,0},{20,4},{24,8},{28,12},{1,17},{... | collective-permute-start | bytes 153608 | tf_op jit(solution)/shard_map/ppermute | solution.py:270
  29.5 3.0 %collective-permute-start.4 = (f32[50,512]{1,0:T(8,128)S(1)}, f32[50,512]{1,0:T(8,128)}, u32[]{:S(2)}, u32[]{:S(2)}) collective-permute-start(f32[50,512]{1,0:T(8,128)S(1)} %maximum_select_fusion.4), channel_id=1, source_target_pairs={{0,8},{4,12},{8,0},{12,4},{16,24},{20,28},{24,16},{28,20},{1,9},{5... | collective-permute-start | bytes 307208 | tf_op jit(solution)/shard_map/ppermute | solution.py:270
  32.6 2.8 %collective-permute-done.4 = f32[50,512]{1,0:T(8,128)} collective-permute-done((f32[50,512]{1,0:T(8,128)S(1)}, f32[50,512]{1,0:T(8,128)}, u32[]{:S(2)}, u32[]{:S(2)}) %collective-permute-start.4) | collective-permute-done | bytes 102432 | tf_op jit(solution)/shard_map/ppermute | solution.py:270
  36.4 1.8 %collective-permute-start.5 = (f32[50,1024]{1,0:T(8,128)S(1)}, f32[50,1024]{1,0:T(8,128)S(1)}, u32[]{:S(2)}, u32[]{:S(2)}) collective-permute-start(f32[50,1024]{1,0:T(8,128)S(1)} %maximum_select_fusion.2.marks_ref), channel_id=1, source_target_pairs={{0,4},{4,0},{8,12},{12,8},{16,20},{20,16},{24,28},{28,24},{1,5},{5... | collective-permute-start | bytes 614408 | tf_op jit(solution)/shard_map/ppermute | solution.py:270
  38.3 8.9 %gather_block.3 = f32[16,1024]{1,0:T(8,128)S(1)} custom-call(bf16[384,4096]{1,0:T(8,128)(2,1)S(1)} %prepare.1.paths_ref.right_ref, f32[50,1024]{1,0:T(8,128)S(1)} %maximum_select_fusion.2.marks_ref, f32[16,4096]{1,0:T(8,128)S(1)} %pad_maximum_fusion.values_ref), custom_call_target="tpu_custom_call" | custom-call | flops 6442450944 | bytes 6291456 | tf_op jit(solution)/shard_map/gather_block/pallas_call | solution.py:107
  47.1 8.9 %gather_block.2 = f32[16,1024]{1,0:T(8,128)S(1)} custom-call(bf16[384,4096]{1,0:T(8,128)(2,1)S(1)} %prepare.1.paths_ref.right_ref, f32[50,1024]{1,0:T(8,128)S(1)} %collective-permute-done.5.marks_ref, f32[16,4096]{1,0:T(8,128)S(1)} %pad_maximum_fusion.values_ref), custom_call_target="tpu_custom_call" | custom-call | flops 6442450944 | bytes 6291456 | tf_op jit(solution)/shard_map/gather_block/pallas_call | solution.py:107
  56.1 3.0 %build_features.5.refs_1_ = bf16[2,512,4096]{2,1,0:T(8,128)(2,1)S(1)} custom-call(f32[50,512]{1,0:T(8,128)S(1)} %get-tuple-element.23.marks_ref, bf16[384,4096]{1,0:T(8,128)(2,1)S(1)} %prepare.1.paths_ref.right_ref), custom_call_target="tpu_custom_call" | custom-call | flops 1610612736 | bytes 16777216 | tf_op jit(solution)/shard_map/build_features/pallas_call | solution.py:180
  59.4 3.0 %build_features.6.refs_2_ = bf16[2,512,4096]{2,1,0:T(8,128)(2,1)S(1)} custom-call(f32[50,512]{1,0:T(8,128)S(1)} %get-tuple-element.22.marks_ref, bf16[384,4096]{1,0:T(8,128)(2,1)S(1)} %prepare.1.paths_ref.right_ref), custom_call_target="tpu_custom_call" | custom-call | flops 1610612736 | bytes 16777216 | tf_op jit(solution)/shard_map/build_features/pallas_call | solution.py:180
  64.2 2.1 %collective-permute-start.7 = (f32[16,2048]{1,0:T(8,128)S(1)}, f32[16,2048]{1,0:T(8,128)S(1)}, u32[]{:S(2)}, u32[]{:S(2)}) collective-permute-start(f32[16,2048]{1,0:T(8,128)S(1)} %add.81), channel_id=1, source_target_pairs={{0,8},{4,12},{8,0},{12,4},{16,24},{20,28},{24,16},{28,20},{1,9},{5... | collective-permute-start | bytes 393224 | tf_op jit(solution)/shard_map/ppermute | solution.py:270
  66.3 3.0 %build_features.7.refs_3_ = bf16[2,512,4096]{2,1,0:T(8,128)(2,1)S(1)} custom-call(f32[50,512]{1,0:T(8,128)S(1)} %get-tuple-element.21.marks_ref, bf16[384,4096]{1,0:T(8,128)(2,1)S(1)} %prepare.1.paths_ref.right_ref), custom_call_target="tpu_custom_call" | custom-call | flops 1610612736 | bytes 16777216 | tf_op jit(solution)/shard_map/build_features/pallas_call | solution.py:180
  69.7 2.0 %collective-permute-start.8 = (f32[16,2048]{1,0:T(8,128)S(1)}, f32[16,2048]{1,0:T(8,128)S(1)}, u32[]{:S(2)}, u32[]{:S(2)}) collective-permute-start(f32[16,2048]{1,0:T(8,128)S(1)} %add.82), channel_id=1, source_target_pairs={{0,16},{4,20},{8,24},{12,28},{16,0},{20,4},{24,8},{28,12},{1,17},{... | collective-permute-start | bytes 393224 | tf_op jit(solution)/shard_map/ppermute | solution.py:270
  71.7 3.2 %build_features.4.refs_0_ = bf16[2,512,4096]{2,1,0:T(8,128)(2,1)S(1)} custom-call(f32[50,512]{1,0:T(8,128)S(1)} %get-tuple-element.24.marks_ref, bf16[384,4096]{1,0:T(8,128)(2,1)S(1)} %prepare.1.paths_ref.right_ref), custom_call_target="tpu_custom_call" | custom-call | flops 1610612736 | bytes 16777216 | tf_op jit(solution)/shard_map/build_features/pallas_call | solution.py:180
  74.9 2.1 %collective-permute-done.8 = f32[16,2048]{1,0:T(8,128)S(1)} collective-permute-done((f32[16,2048]{1,0:T(8,128)S(1)}, f32[16,2048]{1,0:T(8,128)S(1)}, u32[]{:S(2)}, u32[]{:S(2)}) %collective-permute-start.8) | collective-permute-done | bytes 131104 | tf_op jit(solution)/shard_map/ppermute | solution.py:270
  77.0 2.8 %spread_half.5 = f32[16,2176]{1,0:T(8,128)S(1)} custom-call(s32[1]{0:T(128)S(6)} %sub.25.half_ref, f32[16,2048]{1,0:T(8,128)S(1)} %broadcast_multiply_fusion.1.values_ref.other_ref, f32[16,2048]{1,0:T(8,128)S(1)} %broadcast_multiply_fusion.1.values_ref.other_ref, bf16[2,512,4096]{2,1,0:T(8,128)(2,1)S(1)} %build_features.4.refs_0_, ...), custom_call_target="tpu_custom_call" | custom-call | tf_op jit(solution)/shard_map/spread_half/pallas_call | solution.py:218
  79.8 2.8 %spread_half.4 = f32[16,2176]{1,0:T(8,128)S(1)} custom-call(s32[1]{0:T(128)} %bitcast.half_ref, f32[16,2048]{1,0:T(8,128)S(1)} %broadcast_multiply_fusion.1.values_ref.other_ref, f32[16,2048]{1,0:T(8,128)S(1)} %broadcast_multiply_fusion.1.values_ref.other_ref, bf16[2,512,4096]{2,1,0:T(8,128)(2,1)S(1)} %build_features.4.refs_0_, ...), custom_call_target="tpu_custom_call" | custom-call | tf_op jit(solution)/shard_map/spread_half/pallas_call | solution.py:218
  84.1 4.6 %collective-permute-done.10 = f32[16,2176]{1,0:T(8,128)S(1)} collective-permute-done((f32[16,2176]{1,0:T(8,128)S(1)}, f32[16,2176]{1,0:T(8,128)S(1)}, u32[]{:S(2)}, u32[]{:S(2)}) %collective-permute-start.10) | collective-permute-done | bytes 139296 | tf_op jit(solution)/shard_map/ppermute | solution.py:270
  88.9 4.9 %gather_half.2.from_ref = f32[16,2176]{1,0:T(8,128)S(1)} custom-call(s32[1]{0:T(128)} %bitcast.half_ref, f32[16,2048]{1,0:T(8,128)S(1)} %slice_multiply_fusion.2.values_ref, f32[16,2176]{1,0:T(8,128)S(1)} %broadcast_in_dim.10.from_ref, bf16[2,512,4096]{2,1,0:T(8,128)(2,1)S(1)} %build_features.4.refs_0_, bf16[2,512,4096]{2,1,0:T(8,128)(2,1)S(1)} %build_features.5.refs_1_, ...), custom_call_target="tpu_custom_call" | custom-call | flops 3221225472 | bytes 16777216 | tf_op jit(solution)/shard_map/gather_half/pallas_call | solution.py:253
  93.8 4.9 %gather_half.3 = f32[16,2176]{1,0:T(8,128)S(1)} custom-call(s32[1]{0:T(128)S(6)} %sub.25.half_ref, f32[16,2048]{1,0:T(8,128)S(1)} %collective-permute-done.11.values_ref, f32[16,2176]{1,0:T(8,128)S(1)} %gather_half.2.from_ref, bf16[2,512,4096]{2,1,0:T(8,128)(2,1)S(1)} %build_features.4.refs_0_, bf16[2,512,4096]{2,1,0:T(8,128)(2,1)S(1)} %build_features.5.refs_1_, ...), custom_call_target="tpu_custom_call" | custom-call | flops 3221225472 | bytes 16777216 | tf_op jit(solution)/shard_map/gather_half/pallas_call | solution.py:253
  99.2 5.5 %collective-permute-done.12 = f32[16,2176]{1,0:T(8,128)S(1)} collective-permute-done((f32[16,2176]{1,0:T(8,128)S(1)}, f32[16,2176]{1,0:T(8,128)S(1)}, u32[]{:S(2)}, u32[]{:S(2)}) %collective-permute-start.12) | collective-permute-done | bytes 139296 | tf_op jit(solution)/shard_map/ppermute | solution.py:270
  105.1 5.0 %collective-permute-done.13 = f32[16,2176]{1,0:T(8,128)S(1)} collective-permute-done((f32[16,2176]{1,0:T(8,128)S(1)}, f32[16,2176]{1,0:T(8,128)S(1)}, u32[]{:S(2)}, u32[]{:S(2)}) %collective-permute-start.13) | collective-permute-done | bytes 139296 | tf_op jit(solution)/shard_map/ppermute | solution.py:270
  111.9 6.6 %collective-permute-done.14 = f32[16,2176]{1,0:T(8,128)S(1)} collective-permute-done((f32[16,2176]{1,0:T(8,128)S(1)}, f32[16,2176]{1,0:T(8,128)S(1)}, u32[]{:S(2)}, u32[]{:S(2)}) %collective-permute-start.14) | collective-permute-done | bytes 139296 | tf_op jit(solution)/shard_map/ppermute | solution.py:270
  118.7 2.9 %spread_half.7 = f32[16,2176]{1,0:T(8,128)S(1)} custom-call(s32[1]{0:T(128)S(6)} %sub.25.half_ref, f32[16,2048]{1,0:T(8,128)S(1)} %fusion.2.values_ref, f32[16,2048]{1,0:T(8,128)S(1)} %broadcast_multiply_fusion.1.values_ref.other_ref, bf16[2,512,4096]{2,1,0:T(8,128)(2,1)S(1)} %build_features.4.refs_0_, bf16[2,512,4096]{2,1,0:T(8,128)(2,1)S(1)} %build_features.5.refs_1_, ...), custom_call_target="tpu_custom_call" | custom-call | tf_op jit(solution)/shard_map/spread_half/pallas_call | solution.py:218
  121.7 2.8 %spread_half.6 = f32[16,2176]{1,0:T(8,128)S(1)} custom-call(s32[1]{0:T(128)} %bitcast.half_ref, f32[16,2048]{1,0:T(8,128)S(1)} %fusion.2.values_ref, f32[16,2048]{1,0:T(8,128)S(1)} %broadcast_multiply_fusion.1.values_ref.other_ref, bf16[2,512,4096]{2,1,0:T(8,128)(2,1)S(1)} %build_features.4.refs_0_, bf16[2,512,4096]{2,1,0:T(8,128)(2,1)S(1)} %build_features.5.refs_1_, ...), custom_call_target="tpu_custom_call" | custom-call | tf_op jit(solution)/shard_map/spread_half/pallas_call | solution.py:218
  126.0 4.6 %collective-permute-done.16 = f32[16,2176]{1,0:T(8,128)S(1)} collective-permute-done((f32[16,2176]{1,0:T(8,128)S(1)}, f32[16,2176]{1,0:T(8,128)S(1)}, u32[]{:S(2)}, u32[]{:S(2)}) %collective-permute-start.16) | collective-permute-done | bytes 139296 | tf_op jit(solution)/shard_map/ppermute | solution.py:270
  133.0 3.1 %collective-permute-done.18 = f32[16,128]{1,0:T(8,128)S(1)} collective-permute-done((f32[16,128]{1,0:T(8,128)S(1)}, f32[16,128]{1,0:T(8,128)S(1)}, u32[]{:S(2)}, u32[]{:S(2)}) %collective-permute-start.18) | collective-permute-done | bytes 8224 | tf_op jit(solution)/shard_map/ppermute | solution.py:270
  136.2 3.6 %collective-permute-done.19 = f32[16,128]{1,0:T(8,128)S(1)} collective-permute-done((f32[16,128]{1,0:T(8,128)S(1)}, f32[16,128]{1,0:T(8,128)S(1)}, u32[]{:S(2)}, u32[]{:S(2)}) %collective-permute-start.19) | collective-permute-done | bytes 8224 | tf_op jit(solution)/shard_map/ppermute | solution.py:270
  141.3 3.2 %collective-permute-done.20 = f32[16,128]{1,0:T(8,128)S(1)} collective-permute-done((f32[16,128]{1,0:T(8,128)S(1)}, f32[16,128]{1,0:T(8,128)S(1)}, u32[]{:S(2)}, u32[]{:S(2)}) %collective-permute-start.20) | collective-permute-done | bytes 8224 | tf_op jit(solution)/shard_map/ppermute | solution.py:270
  (74 shorter events, 25.9 us)
Async XLA Ops:
  0.0 32.5 %copy-start.4 = (f32[4096]{0:T(1024)S(1)}, f32[4096]{0:T(1024)}, u32[]{:S(2)}) copy-start(f32[4096]{0:T(1024)} %param.5) | copy-start | bytes 49156
  0.7 1.2 copy-start
  1.9 25.1 %copy-start.3 = (f32[15,4096]{1,0:T(8,128)S(1)}, f32[15,4096]{1,0:T(8,128)}, u32[]{:S(2)}) copy-start(f32[15,4096]{1,0:T(8,128)} %param.6) | copy-start | bytes 737284
  5.3 8.7 %collective-permute-start = (f32[50,1024]{1,0:T(8,128)S(1)}, f32[50,1024]{1,0:T(8,128)S(1)}, u32[]{:S(2)}, u32[]{:S(2)}) collective-permute-start(f32[50,1024]{1,0:T(8,128)S(1)} %pick.2), channel_id=1, source_target_pairs={{0,4},{4,0},{8,12},{12,8},{16,20},{20,16},{24,28},{28,24},{1,5},{5... | collective-permute-start | bytes 614408 | tf_op jit(solution)/shard_map/ppermute | solution.py:270
  9.1 1.2 copy-start.1
  14.0 4.9 %collective-permute-start.1 = (f32[50,512]{1,0:T(8,128)S(1)}, f32[50,512]{1,0:T(8,128)S(1)}, u32[]{:S(2)}, u32[]{:S(2)}) collective-permute-start(f32[50,512]{1,0:T(8,128)S(1)} %slice_select_fusion), channel_id=1, source_target_pairs={{0,8},{4,12},{8,0},{12,4},{16,24},{20,28},{24,16},{28,20},{1,9},{5... | collective-permute-start | bytes 307208 | tf_op jit(solution)/shard_map/ppermute | solution.py:270
  18.9 5.3 %collective-permute-start.2 = (f32[50,256]{1,0:T(8,128)S(1)}, f32[50,256]{1,0:T(8,128)S(1)}, u32[]{:S(2)}, u32[]{:S(2)}) collective-permute-start(f32[50,256]{1,0:T(8,128)S(1)} %get-tuple-element.25), channel_id=1, source_target_pairs={{0,16},{4,20},{8,24},{12,28},{16,0},{20,4},{24,8},{28,12},{1,17},{... | collective-permute-start | bytes 153608 | tf_op jit(solution)/shard_map/ppermute | solution.py:270
  21.8 1.2 copy-start.2
  24.3 5.2 %collective-permute-start.3 = (f32[50,256]{1,0:T(8,128)S(1)}, f32[50,256]{1,0:T(8,128)S(1)}, u32[]{:S(2)}, u32[]{:S(2)}) collective-permute-start(f32[50,256]{1,0:T(8,128)S(1)} %add.80), channel_id=1, source_target_pairs={{0,16},{4,20},{8,24},{12,28},{16,0},{20,4},{24,8},{28,12},{1,17},{... | collective-permute-start | bytes 153608 | tf_op jit(solution)/shard_map/ppermute | solution.py:270
  29.5 5.9 %collective-permute-start.4 = (f32[50,512]{1,0:T(8,128)S(1)}, f32[50,512]{1,0:T(8,128)}, u32[]{:S(2)}, u32[]{:S(2)}) collective-permute-start(f32[50,512]{1,0:T(8,128)S(1)} %maximum_select_fusion.4), channel_id=1, source_target_pairs={{0,8},{4,12},{8,0},{12,4},{16,24},{20,28},{24,16},{28,20},{1,9},{5... | collective-permute-start | bytes 307208 | tf_op jit(solution)/shard_map/ppermute | solution.py:270
  36.4 10.7 %collective-permute-start.5 = (f32[50,1024]{1,0:T(8,128)S(1)}, f32[50,1024]{1,0:T(8,128)S(1)}, u32[]{:S(2)}, u32[]{:S(2)}) collective-permute-start(f32[50,1024]{1,0:T(8,128)S(1)} %maximum_select_fusion.2.marks_ref), channel_id=1, source_target_pairs={{0,4},{4,0},{8,12},{12,8},{16,20},{20,16},{24,28},{28,24},{1,5},{5... | collective-permute-start | bytes 614408 | tf_op jit(solution)/shard_map/ppermute | solution.py:270
  59.1 5.0 %collective-permute-start.6 = (f32[16,2048]{1,0:T(8,128)S(1)}, f32[16,2048]{1,0:T(8,128)S(1)}, u32[]{:S(2)}, u32[]{:S(2)}) collective-permute-start(f32[16,2048]{1,0:T(8,128)S(1)} %maximum_select_fusion.3), channel_id=1, source_target_pairs={{0,4},{4,0},{8,12},{12,8},{16,20},{20,16},{24,28},{28,24},{1,5},{5... | collective-permute-start | bytes 393224 | tf_op jit(solution)/shard_map/ppermute | solution.py:270
  64.2 5.5 %collective-permute-start.7 = (f32[16,2048]{1,0:T(8,128)S(1)}, f32[16,2048]{1,0:T(8,128)S(1)}, u32[]{:S(2)}, u32[]{:S(2)}) collective-permute-start(f32[16,2048]{1,0:T(8,128)S(1)} %add.81), channel_id=1, source_target_pairs={{0,8},{4,12},{8,0},{12,4},{16,24},{20,28},{24,16},{28,20},{1,9},{5... | collective-permute-start | bytes 393224 | tf_op jit(solution)/shard_map/ppermute | solution.py:270
  69.7 7.3 %collective-permute-start.8 = (f32[16,2048]{1,0:T(8,128)S(1)}, f32[16,2048]{1,0:T(8,128)S(1)}, u32[]{:S(2)}, u32[]{:S(2)}) collective-permute-start(f32[16,2048]{1,0:T(8,128)S(1)} %add.82), channel_id=1, source_target_pairs={{0,16},{4,20},{8,24},{12,28},{16,0},{20,4},{24,8},{28,12},{1,17},{... | collective-permute-start | bytes 393224 | tf_op jit(solution)/shard_map/ppermute | solution.py:270
  79.8 2.8 %collective-permute-start.9 = (f32[16,2176]{1,0:T(8,128)S(1)}, f32[16,2176]{1,0:T(8,128)S(1)}, u32[]{:S(2)}, u32[]{:S(2)}) collective-permute-start(f32[16,2176]{1,0:T(8,128)S(1)} %spread_half.5), channel_id=1, source_target_pairs={{0,1},{1,0},{2,3},{3,2},{4,5},{5,4},{6,7},{7,6},{8,9},{9,8},{10,11... | collective-permute-start | bytes 417800 | tf_op jit(solution)/shard_map/ppermute | solution.py:270
  82.6 6.1 %collective-permute-start.10 = (f32[16,2176]{1,0:T(8,128)S(1)}, f32[16,2176]{1,0:T(8,128)S(1)}, u32[]{:S(2)}, u32[]{:S(2)}) collective-permute-start(f32[16,2176]{1,0:T(8,128)S(1)} %add.84), channel_id=1, source_target_pairs={{0,2},{1,3},{2,0},{3,1},{4,6},{5,7},{6,4},{7,5},{8,10},{9,11},{10,... | collective-permute-start | bytes 417800 | tf_op jit(solution)/shard_map/ppermute | solution.py:270
  88.8 5.0 %collective-permute-start.11 = (f32[16,2048]{1,0:T(8,128)S(1)}, f32[16,2048]{1,0:T(8,128)S(1)}, u32[]{:S(2)}, u32[]{:S(2)}) collective-permute-start(f32[16,2048]{1,0:T(8,128)S(1)} %slice_multiply_fusion.2.values_ref), channel_id=1, source_target_pairs={{0,1},{1,0},{2,3},{3,2},{4,5},{5,4},{6,7},{7,6},{8,9},{9,8},{10,11... | collective-permute-start | bytes 393224 | tf_op jit(solution)/shard_map/ppermute | solution.py:270
  98.6 6.1 %collective-permute-start.12 = (f32[16,2176]{1,0:T(8,128)S(1)}, f32[16,2176]{1,0:T(8,128)S(1)}, u32[]{:S(2)}, u32[]{:S(2)}) collective-permute-start(f32[16,2176]{1,0:T(8,128)S(1)} %gather_half.3), channel_id=1, source_target_pairs={{0,4},{4,0},{8,12},{12,8},{16,20},{20,16},{24,28},{28,24},{1,5},{5... | collective-permute-start | bytes 417800 | tf_op jit(solution)/shard_map/ppermute | solution.py:270
  104.7 5.4 %collective-permute-start.13 = (f32[16,2176]{1,0:T(8,128)S(1)}, f32[16,2176]{1,0:T(8,128)S(1)}, u32[]{:S(2)}, u32[]{:S(2)}) collective-permute-start(f32[16,2176]{1,0:T(8,128)S(1)} %add.86), channel_id=1, source_target_pairs={{0,8},{4,12},{8,0},{12,4},{16,24},{20,28},{24,16},{28,20},{1,9},{5... | collective-permute-start | bytes 417800 | tf_op jit(solution)/shard_map/ppermute | solution.py:270
  110.1 8.4 %collective-permute-start.14 = (f32[16,2176]{1,0:T(8,128)S(1)}, f32[16,2176]{1,0:T(8,128)S(1)}, u32[]{:S(2)}, u32[]{:S(2)}) collective-permute-start(f32[16,2176]{1,0:T(8,128)S(1)} %add.87), channel_id=1, source_target_pairs={{0,16},{4,20},{8,24},{12,28},{16,0},{20,4},{24,8},{28,12},{1,17},{... | collective-permute-start | bytes 417800 | tf_op jit(solution)/shard_map/ppermute | solution.py:270
  121.6 2.8 %collective-permute-start.15 = (f32[16,2176]{1,0:T(8,128)S(1)}, f32[16,2176]{1,0:T(8,128)S(1)}, u32[]{:S(2)}, u32[]{:S(2)}) collective-permute-start(f32[16,2176]{1,0:T(8,128)S(1)} %spread_half.7), channel_id=1, source_target_pairs={{0,1},{1,0},{2,3},{3,2},{4,5},{5,4},{6,7},{7,6},{8,9},{9,8},{10,11... | collective-permute-start | bytes 417800 | tf_op jit(solution)/shard_map/ppermute | solution.py:270
  124.5 6.1 %collective-permute-start.16 = (f32[16,2176]{1,0:T(8,128)S(1)}, f32[16,2176]{1,0:T(8,128)S(1)}, u32[]{:S(2)}, u32[]{:S(2)}) collective-permute-start(f32[16,2176]{1,0:T(8,128)S(1)} %add.91), channel_id=1, source_target_pairs={{0,2},{1,3},{2,0},{3,1},{4,6},{5,7},{6,4},{7,5},{8,10},{9,11},{10,... | collective-permute-start | bytes 417800 | tf_op jit(solution)/shard_map/ppermute | solution.py:270
  130.7 1.4 collective-permute-start.17
  132.4 3.7 %collective-permute-start.18 = (f32[16,128]{1,0:T(8,128)S(1)}, f32[16,128]{1,0:T(8,128)S(1)}, u32[]{:S(2)}, u32[]{:S(2)}) collective-permute-start(f32[16,128]{1,0:T(8,128)S(1)} %broadcast_in_dim.22), channel_id=1, source_target_pairs={{0,4},{4,0},{8,12},{12,8},{16,20},{20,16},{24,28},{28,24},{1,5},{5... | collective-permute-start | bytes 24584 | tf_op jit(solution)/shard_map/ppermute | solution.py:270
  136.2 3.7 %collective-permute-start.19 = (f32[16,128]{1,0:T(8,128)S(1)}, f32[16,128]{1,0:T(8,128)S(1)}, u32[]{:S(2)}, u32[]{:S(2)}) collective-permute-start(f32[16,128]{1,0:T(8,128)S(1)} %broadcast_add_fusion), channel_id=1, source_target_pairs={{0,8},{4,12},{8,0},{12,4},{16,24},{20,28},{24,16},{28,20},{1,9},{5... | collective-permute-start | bytes 24584 | tf_op jit(solution)/shard_map/ppermute | solution.py:270
  139.9 4.6 %collective-permute-start.20 = (f32[16,128]{1,0:T(8,128)S(1)}, f32[16,128]{1,0:T(8,128)S(1)}, u32[]{:S(2)}, u32[]{:S(2)}) collective-permute-start(f32[16,128]{1,0:T(8,128)S(1)} %fusion.15), channel_id=1, source_target_pairs={{0,16},{4,20},{8,24},{12,28},{16,0},{20,4},{24,8},{28,12},{1,17},{... | collective-permute-start | bytes 24584 | tf_op jit(solution)/shard_map/ppermute | solution.py:270
